TPU v7x, 128 devices: a whole 4x4x4 slice. The times are simulated.
128 devices in a mesh: gx: 4 (over y), gy: 32 (over z, x, core).
Axes of the slice: x: 4, y: 4, z: 4, core: 2. Of those that a mesh axis runs over, the one named last changes fastest.
Arguments:
- cam_pose: float32 [7, 32768], P(None, ('gx', 'gy')), may hold values from -0.5 to 2, as said below
- points: float32 [3, 524288], P(None, ('gx', 'gy')), may hold values from -1.5 to 8, as said below
- obs_uv: float32 [2, 128, 128, 128], P(None, ('gx', 'gy')), may hold values from -0.6 to 0.6
- obs_cam: int32 [128, 128, 128], P(('gx', 'gy')), may hold values from 0 to 255
- obs_pt: int32 [128, 128, 128], P(('gx', 'gy')), may hold values from 0 to 4095
- block_count: int32 [128, 128], P(('gx', 'gy')), may hold values from 1 to 128, as said below
- send_list: int32 [128, 128, 16], P(('gx', 'gy')), may hold values from 0 to 255
- edge_slot: int32 [8, 32768], P(None, ('gx', 'gy')), may hold values from 0 to 2047
- edge_weight: float32 [8, 32768], P(None, ('gx', 'gy')), may hold values from 0.2 to 1
Outputs:
- cam_step: float32 [6, 32768], P(None, ('gx', 'gy'))
- cam_residual: float32 [6, 32768], P(None, ('gx', 'gy'))
Inputs may be any that keep to these rules, and one draw needn't show every extreme that they name: `cam_pose`: rows 0 in [0.9, 1.1], rows 1 to 3 in [-0.15, 0.15], rows 4 and 5 in [-0.5, 0.5], row 6 in [1, 2]. `points`: rows 0 and 1 in [-1.5, 1.5], row 2 in [4, 8]. Slot j of block [d, s] is live exactly when j < block_count[d, s]; some blocks are full.
All inputs are finite; a program needn't handle non-finite values.
Results may differ from a plain program's by a relative error of at most 0.00021.
Values sent between devices are 32-bit elements; how exact they have to be, the bound alone decides.
No kernel may reach another device: no remote copies, remote signals or barrier semaphores. Data moves between devices by JAX's collectives and lax.ppermute only.
A program may use at most 64 MiB of HBM per device.

v0:
```python
import math

import jax
import jax.numpy as jnp
from jax import lax
from jax.sharding import Mesh
from jax.sharding import PartitionSpec as P

ITERS = 2
GX_GY = ("gx", "gy_0", "gy_1", "gy_2")
GY = ("gy_0", "gy_1", "gy_2")


DAMPING = 1.0
SYMMETRIC_PAIRS = [(a, b) for a in range(6) for b in range(a, 6)]
POINT_PAIRS = [(0, 0), (0, 1), (0, 2), (1, 1), (1, 2), (2, 2)]


def over_axes(array, axes):
    for axis in axes:
        array = lax.psum(array, axis)
    return array


def pick_columns(table, index):
    count_all = index.shape[0]
    table_width = table.shape[1]
    block_size = math.gcd(count_all, 2048)
    grouped = index.reshape(count_all // block_size, block_size)

    def select(chosen):
        onehot = (
            lax.broadcasted_iota(jnp.int32, (table_width, block_size), 0) == chosen[None, :]
        ).astype(jnp.float32)
        return jnp.dot(
            table, onehot, precision=lax.Precision.HIGHEST, preferred_element_type=jnp.float32
        )

    picked = lax.map(select, grouped)
    return jnp.transpose(picked, (1, 0, 2)).reshape(table.shape[0], count_all)


def add_columns(values, index, table_width):
    row_count, count_all = values.shape
    block_size = math.gcd(count_all, 2048)
    blocks_all = count_all // block_size
    grouped = index.reshape(blocks_all, block_size)
    pieces = jnp.transpose(values.reshape(row_count, blocks_all, block_size), (1, 0, 2))

    def accumulate(carry, item):
        piece, chosen = item
        onehot = (
            lax.broadcasted_iota(jnp.int32, (table_width, block_size), 0) == chosen[None, :]
        ).astype(jnp.float32)
        added = lax.dot_general(
            piece,
            onehot,
            (((1,), (1,)), ((), ())),
            precision=lax.Precision.HIGHEST,
            preferred_element_type=jnp.float32,
        )
        return (carry + added, None)

    summed, _ = lax.scan(
        accumulate, jnp.zeros((row_count, table_width), jnp.float32), (pieces, grouped)
    )
    return summed


def rotation(quaternion):
    q0, q1, q2, q3 = (quaternion[0], quaternion[1], quaternion[2], quaternion[3])
    inverse_norm = 1.0 / (q0 * q0 + q1 * q1 + q2 * q2 + q3 * q3)
    entries = [
        q0 * q0 + q1 * q1 - q2 * q2 - q3 * q3,
        2.0 * (q1 * q2 - q0 * q3),
        2.0 * (q1 * q3 + q0 * q2),
        2.0 * (q1 * q2 + q0 * q3),
        q0 * q0 - q1 * q1 + q2 * q2 - q3 * q3,
        2.0 * (q2 * q3 - q0 * q1),
        2.0 * (q1 * q3 - q0 * q2),
        2.0 * (q2 * q3 + q0 * q1),
        q0 * q0 - q1 * q1 - q2 * q2 + q3 * q3,
    ]
    return jnp.stack([value * inverse_norm for value in entries])


def eliminate(measured, rot_rows, translation, point_rows, live_mask, point_index, count_points):
    cam_pt = [
        rot_rows[3 * a] * point_rows[0]
        + rot_rows[3 * a + 1] * point_rows[1]
        + rot_rows[3 * a + 2] * point_rows[2]
        + translation[a]
        for a in range(3)
    ]
    inv_depth = 1.0 / cam_pt[2]
    proj_u = cam_pt[0] * inv_depth
    proj_v = cam_pt[1] * inv_depth
    residue = [(proj_u - measured[0]) * live_mask, (proj_v - measured[1]) * live_mask]
    scaled = inv_depth * live_mask
    zeros_row = jnp.zeros_like(scaled)
    jac_proj = [[scaled, zeros_row, -proj_u * scaled], [zeros_row, scaled, -proj_v * scaled]]
    cross_matrix = [
        [zeros_row, cam_pt[2], -cam_pt[1]],
        [-cam_pt[2], zeros_row, cam_pt[0]],
        [cam_pt[1], -cam_pt[0], zeros_row],
    ]
    jac_cam = []
    jac_point = []
    for i in range(2):
        jac_row = [
            jac_proj[i][0] * cross_matrix[0][k]
            + jac_proj[i][1] * cross_matrix[1][k]
            + jac_proj[i][2] * cross_matrix[2][k]
            for k in range(3)
        ]
        jac_cam.append(jac_row + jac_proj[i])
        jac_point.append(
            [
                jac_proj[i][0] * rot_rows[k]
                + jac_proj[i][1] * rot_rows[3 + k]
                + jac_proj[i][2] * rot_rows[6 + k]
                for k in range(3)
            ]
        )
    point_terms = [
        jac_point[0][k] * jac_point[0][l] + jac_point[1][k] * jac_point[1][l]
        for k, l in POINT_PAIRS
    ]
    point_terms = point_terms + [
        jac_point[0][k] * residue[0] + jac_point[1][k] * residue[1] for k in range(3)
    ]
    point_sums = add_columns(jnp.stack(point_terms), point_index, count_points)
    hess = [
        point_sums[0] + DAMPING,
        point_sums[1],
        point_sums[2],
        point_sums[3] + DAMPING,
        point_sums[4],
        point_sums[5] + DAMPING,
    ]
    cofactor = [
        hess[3] * hess[5] - hess[4] * hess[4],
        hess[2] * hess[4] - hess[1] * hess[5],
        hess[1] * hess[4] - hess[2] * hess[3],
        hess[0] * hess[5] - hess[2] * hess[2],
        hess[1] * hess[2] - hess[0] * hess[4],
        hess[0] * hess[3] - hess[1] * hess[1],
    ]
    determinant = hess[0] * cofactor[0] + hess[1] * cofactor[1] + hess[2] * cofactor[2]
    per_point = pick_columns(
        jnp.stack(
            [value / determinant for value in cofactor]
            + [point_sums[6], point_sums[7], point_sums[8]]
        ),
        point_index,
    )
    inv_full = [
        [per_point[0], per_point[1], per_point[2]],
        [per_point[1], per_point[3], per_point[4]],
        [per_point[2], per_point[4], per_point[5]],
    ]
    grad_point = [per_point[6], per_point[7], per_point[8]]
    coupling = [
        [jac_cam[0][a] * jac_point[0][k] + jac_cam[1][a] * jac_point[1][k] for k in range(3)]
        for a in range(6)
    ]
    coupled = [
        [
            coupling[a][0] * inv_full[0][k]
            + coupling[a][1] * inv_full[1][k]
            + coupling[a][2] * inv_full[2][k]
            for k in range(3)
        ]
        for a in range(6)
    ]
    schur_block = [
        jac_cam[0][a] * jac_cam[0][b]
        + jac_cam[1][a] * jac_cam[1][b]
        - (
            coupled[a][0] * coupling[b][0]
            + coupled[a][1] * coupling[b][1]
            + coupled[a][2] * coupling[b][2]
        )
        for a, b in SYMMETRIC_PAIRS
    ]
    reduced = [
        jac_cam[0][a] * residue[0]
        + jac_cam[1][a] * residue[1]
        - (
            coupled[a][0] * grad_point[0]
            + coupled[a][1] * grad_point[1]
            + coupled[a][2] * grad_point[2]
        )
        for a in range(6)
    ]
    return jnp.stack(schur_block + reduced)


def block_product(blocks, vector):
    lookup = {}
    for index, (a, b) in enumerate(SYMMETRIC_PAIRS):
        lookup[a, b] = index
        lookup[b, a] = index
    return jnp.stack([sum((blocks[lookup[a, b]] * vector[b] for b in range(6))) for a in range(6)])


def send_observations(payload):
    return lax.all_to_all(payload, GX_GY, split_axis=1, concat_axis=1, tiled=True)


def send_results(payload):
    return lax.all_to_all(payload, GX_GY, split_axis=1, concat_axis=1, tiled=True)


def global_sum(value):
    return over_axes(value, GX_GY)


def per_device(
    cam_pose, points, obs_uv, obs_cam, obs_pt, block_count, send_list, edge_slot, edge_weight
):
    devices = lax.axis_size("gx") * lax.axis_size(GY)
    slot_width = obs_uv.shape[-1]
    cam_dev = cam_pose.shape[1]
    pt_dev = points.shape[1]
    cam_index = obs_cam.reshape(-1)
    measured = obs_uv.reshape(2, -1)
    posed = pick_columns(jnp.concatenate([rotation(cam_pose[0:4]), cam_pose[4:7]], 0), cam_index)
    payload = jnp.concatenate([measured, posed], 0)
    arrived = send_observations(payload)
    rot_rows = arrived[2:11]
    moved_translation = arrived[11:14]
    live_count = block_count.reshape(-1)
    position = lax.broadcasted_iota(jnp.int32, (devices, slot_width), 1)
    live_mask = (position < live_count[:, None]).astype(jnp.float32).reshape(-1)
    point_index = obs_pt.reshape(-1)
    point_rows = pick_columns(points, point_index)
    entries = eliminate(
        arrived[0:2], rot_rows, moved_translation, point_rows, live_mask, point_index, pt_dev
    )
    returned = send_results(entries)
    camera_sums = add_columns(returned, cam_index, cam_dev)
    blocks = camera_sums[0:21]
    gradient = camera_sums[21:27]
    send_index = send_list.reshape(-1)
    flat_slots = edge_slot.reshape(-1)
    diagonal_entries = (
        jnp.stack([blocks[SYMMETRIC_PAIRS.index((a, a))] for a in range(6)]) + DAMPING
    )
    update_step = jnp.zeros((6, cam_dev), jnp.float32)
    residual = -gradient
    precond = residual / diagonal_entries
    direction = precond
    precond_dot = global_sum(jnp.sum(residual * precond))
    for iteration in range(ITERS):
        outgoing = pick_columns(direction, send_index)
        incoming = lax.all_to_all(outgoing, GX_GY, split_axis=1, concat_axis=1, tiled=True)
        nearby = pick_columns(incoming, flat_slots).reshape(
            6, edge_slot.shape[0], edge_slot.shape[1]
        )
        edge_term = edge_weight[None] * (direction[:, None, :] - nearby)
        applied = (
            block_product(blocks, direction) + DAMPING * direction + jnp.sum(edge_term, axis=1)
        )
        slot_sums = add_columns(edge_term.reshape(6, -1), flat_slots, incoming.shape[1])
        flowed = lax.all_to_all(slot_sums, GX_GY, split_axis=1, concat_axis=1, tiled=True)
        product_image = applied - add_columns(flowed, send_index, direction.shape[1])
        step_size = precond_dot / global_sum(jnp.sum(direction * product_image))
        update_step = update_step + step_size * direction
        residual = residual - step_size * product_image
        if iteration + 1 < ITERS:
            precond = residual / diagonal_entries
            next_dot = global_sum(jnp.sum(residual * precond))
            direction = precond + next_dot / precond_dot * direction
            precond_dot = next_dot
    return (update_step, residual)


def solution(mesh):
    finer = Mesh(mesh.devices.reshape(mesh.shape["gx"], 4, 4, 2), ("gx", "gy_0", "gy_1", "gy_2"))
    in_specs = (
        P(None, GX_GY),
        P(None, GX_GY),
        P(None, GX_GY, None, None),
        P(GX_GY, None, None),
        P(GX_GY, None, None),
        P(GX_GY, None),
        P(GX_GY, None, None),
        P(None, GX_GY),
        P(None, GX_GY),
    )
    out_specs = (P(None, GX_GY), P(None, GX_GY))
    return jax.shard_map(
        per_device, mesh=finer, in_specs=in_specs, out_specs=out_specs, check_vma=False
    )
```

profile of v0, /device:TPU:1, one launch (start us, length us, event | category | flops | bytes accessed | tf_op | source)
XLA Modules:
  0.0 606.7 jit_solution(4796119729243833296)
XLA Ops:
  13.6 11.9 %all-to-all-start = ((f32[14,128,128]{2,0,1:T(8,128)}), f32[14,128,128]{2,0,1:T(8,128)S(1)}, u32[]{:S(2)}, u32[]{:S(2)}) async-start(f32[14,128,128]{2,0,1:T(8,128)} %copy.139), calls=%async_computation | async-start | bytes 2097152 | tf_op jit(solution)/shard_map/all_to_all | solution.py:208
  25.6 84.8 %while.13 = (s32[]{:T(128)}, f32[8,3,2048]{2,0,1:T(8,128)S(1)}, s32[8,2048]{1,0:T(8,128)S(1)}, f32[3,4096]{1,0:T(4,128)S(1)}, s32[]{:T(128)}, /*index=5*/s32[]{:T(128)}) while((s32[]{:T(128)}, f32[8,3,2048]{2,0,1:T(8,128)S(1)}, s32[8,2048]{1,0:T(8,128)S(1)}, f32[3,4096]{1,0:T(4,128)S(1)}, s32[]{:T(128)}, /*index=5*/s32[]{:T(128)}) %tuple.239), condition=%wide.region_3.4_spmd, body=%wide.region_2.3_spmd.sunk | while | flops 310378496 | bytes 196685 | solution.py:39
  25.6 10.3 %fusion.65 = f32[1,3,2048]{2,1,0:T(4,128)S(1)} fusion(f32[3,4096]{1,0:T(4,128)S(1)} %get-tuple-element.615, s32[2048]{0:T(1024)S(1)} %bitcast.210), kind=kOutput, calls=%fused_computation.8.clone.1 | convolution fusion | flops 310378496 | bytes 81920 | tf_op jit(solution)/shard_map/while/body/eval_jaxpr/dot_general | solution.py:35
  36.2 10.3 %fusion.65 = f32[1,3,2048]{2,1,0:T(4,128)S(1)} fusion(f32[3,4096]{1,0:T(4,128)S(1)} %get-tuple-element.615, s32[2048]{0:T(1024)S(1)} %bitcast.210), kind=kOutput, calls=%fused_computation.8.clone.1 | convolution fusion | flops 310378496 | bytes 81920 | tf_op jit(solution)/shard_map/while/body/eval_jaxpr/dot_general | solution.py:35
  46.8 10.3 %fusion.65 = f32[1,3,2048]{2,1,0:T(4,128)S(1)} fusion(f32[3,4096]{1,0:T(4,128)S(1)} %get-tuple-element.615, s32[2048]{0:T(1024)S(1)} %bitcast.210), kind=kOutput, calls=%fused_computation.8.clone.1 | convolution fusion | flops 310378496 | bytes 81920 | tf_op jit(solution)/shard_map/while/body/eval_jaxpr/dot_general | solution.py:35
  57.4 10.3 %fusion.65 = f32[1,3,2048]{2,1,0:T(4,128)S(1)} fusion(f32[3,4096]{1,0:T(4,128)S(1)} %get-tuple-element.615, s32[2048]{0:T(1024)S(1)} %bitcast.210), kind=kOutput, calls=%fused_computation.8.clone.1 | convolution fusion | flops 310378496 | bytes 81920 | tf_op jit(solution)/shard_map/while/body/eval_jaxpr/dot_general | solution.py:35
  68.0 10.3 %fusion.65 = f32[1,3,2048]{2,1,0:T(4,128)S(1)} fusion(f32[3,4096]{1,0:T(4,128)S(1)} %get-tuple-element.615, s32[2048]{0:T(1024)S(1)} %bitcast.210), kind=kOutput, calls=%fused_computation.8.clone.1 | convolution fusion | flops 310378496 | bytes 81920 | tf_op jit(solution)/shard_map/while/body/eval_jaxpr/dot_general | solution.py:35
  78.6 10.3 %fusion.65 = f32[1,3,2048]{2,1,0:T(4,128)S(1)} fusion(f32[3,4096]{1,0:T(4,128)S(1)} %get-tuple-element.615, s32[2048]{0:T(1024)S(1)} %bitcast.210), kind=kOutput, calls=%fused_computation.8.clone.1 | convolution fusion | flops 310378496 | bytes 81920 | tf_op jit(solution)/shard_map/while/body/eval_jaxpr/dot_general | solution.py:35
  120.9 127.4 %while.15 = (s32[]{:T(128)}, f32[9,4096]{1,0:T(8,128)S(1)}, f32[8,9,2048]{2,0,1:T(8,128)}, s32[8,2048]{1,0:T(8,128)S(1)}, s32[]{:T(128)}, /*index=5*/s32[]{:T(128)}) while((s32[]{:T(128)}, f32[9,4096]{1,0:T(8,128)S(1)}, f32[8,9,2048]{2,0,1:T(8,128)}, s32[8,2048]{1,0:T(8,128)S(1)}, s32[]{:T(128)}, /*index=5*/s32[]{:T(128)}) %tuple.238), condition=%wide.region_5.6_spmd.clone, body=%wide.region_4.5_spmd.clone.sunk | while | flops 914432000 | bytes 540759 | solution.py:64
  122.6 14.7 %fusion.68 = f32[9,4096]{1,0:T(8,128)S(1)} fusion(s32[2048]{0:T(1024)S(1)} %bitcast.206, f32[9,4096]{1,0:T(8,128)S(1)} %get-tuple-element.625, f32[1,9,2048]{2,0,1:T(1,128)S(1)} %constant_dynamic-slice_fusion.18, pred[]{:T(512)S(6)} %compare.6), kind=kOutput, calls=%fused_computation.19.clone.1 | convolution fusion | flops 914432000 | bytes 376833 | tf_op jit(solution)/shard_map/while/body/eval_jaxpr/dot_general | solution.py:55
  138.5 14.7 %fusion.68 = f32[9,4096]{1,0:T(8,128)S(1)} fusion(s32[2048]{0:T(1024)S(1)} %bitcast.206, f32[9,4096]{1,0:T(8,128)S(1)} %get-tuple-element.625, f32[1,9,2048]{2,0,1:T(1,128)S(1)} %constant_dynamic-slice_fusion.18, pred[]{:T(512)S(6)} %compare.6), kind=kOutput, calls=%fused_computation.19.clone.1 | convolution fusion | flops 914432000 | bytes 376833 | tf_op jit(solution)/shard_map/while/body/eval_jaxpr/dot_general | solution.py:55
  154.3 14.7 %fusion.68 = f32[9,4096]{1,0:T(8,128)S(1)} fusion(s32[2048]{0:T(1024)S(1)} %bitcast.206, f32[9,4096]{1,0:T(8,128)S(1)} %get-tuple-element.625, f32[1,9,2048]{2,0,1:T(1,128)S(1)} %constant_dynamic-slice_fusion.18, pred[]{:T(512)S(6)} %compare.6), kind=kOutput, calls=%fused_computation.19.clone.1 | convolution fusion | flops 914432000 | bytes 376833 | tf_op jit(solution)/shard_map/while/body/eval_jaxpr/dot_general | solution.py:55
  170.2 14.7 %fusion.68 = f32[9,4096]{1,0:T(8,128)S(1)} fusion(s32[2048]{0:T(1024)S(1)} %bitcast.206, f32[9,4096]{1,0:T(8,128)S(1)} %get-tuple-element.625, f32[1,9,2048]{2,0,1:T(1,128)S(1)} %constant_dynamic-slice_fusion.18, pred[]{:T(512)S(6)} %compare.6), kind=kOutput, calls=%fused_computation.19.clone.1 | convolution fusion | flops 914432000 | bytes 376833 | tf_op jit(solution)/shard_map/while/body/eval_jaxpr/dot_general | solution.py:55
  186.0 14.7 %fusion.68 = f32[9,4096]{1,0:T(8,128)S(1)} fusion(s32[2048]{0:T(1024)S(1)} %bitcast.206, f32[9,4096]{1,0:T(8,128)S(1)} %get-tuple-element.625, f32[1,9,2048]{2,0,1:T(1,128)S(1)} %constant_dynamic-slice_fusion.18, pred[]{:T(512)S(6)} %compare.6), kind=kOutput, calls=%fused_computation.19.clone.1 | convolution fusion | flops 914432000 | bytes 376833 | tf_op jit(solution)/shard_map/while/body/eval_jaxpr/dot_general | solution.py:55
  201.9 14.7 %fusion.68 = f32[9,4096]{1,0:T(8,128)S(1)} fusion(s32[2048]{0:T(1024)S(1)} %bitcast.206, f32[9,4096]{1,0:T(8,128)S(1)} %get-tuple-element.625, f32[1,9,2048]{2,0,1:T(1,128)S(1)} %constant_dynamic-slice_fusion.18, pred[]{:T(512)S(6)} %compare.6), kind=kOutput, calls=%fused_computation.19.clone.1 | convolution fusion | flops 914432000 | bytes 376833 | tf_op jit(solution)/shard_map/while/body/eval_jaxpr/dot_general | solution.py:55
  217.8 14.7 %fusion.68 = f32[9,4096]{1,0:T(8,128)S(1)} fusion(s32[2048]{0:T(1024)S(1)} %bitcast.206, f32[9,4096]{1,0:T(8,128)S(1)} %get-tuple-element.625, f32[1,9,2048]{2,0,1:T(1,128)S(1)} %constant_dynamic-slice_fusion.18, pred[]{:T(512)S(6)} %compare.6), kind=kOutput, calls=%fused_computation.19.clone.1 | convolution fusion | flops 914432000 | bytes 376833 | tf_op jit(solution)/shard_map/while/body/eval_jaxpr/dot_general | solution.py:55
  233.6 14.7 %fusion.68 = f32[9,4096]{1,0:T(8,128)S(1)} fusion(s32[2048]{0:T(1024)S(1)} %bitcast.206, f32[9,4096]{1,0:T(8,128)S(1)} %get-tuple-element.625, f32[1,9,2048]{2,0,1:T(1,128)S(1)} %constant_dynamic-slice_fusion.18, pred[]{:T(512)S(6)} %compare.6), kind=kOutput, calls=%fused_computation.19.clone.1 | convolution fusion | flops 914432000 | bytes 376833 | tf_op jit(solution)/shard_map/while/body/eval_jaxpr/dot_general | solution.py:55
  249.0 84.0 %while.14 = (s32[]{:T(128)}, f32[8,9,2048]{2,1,0:T(8,128)S(1)}, s32[8,2048]{1,0:T(8,128)S(1)}, f32[9,4096]{1,0:T(8,128)S(1)}, s32[]{:T(128)}) while((s32[]{:T(128)}, f32[8,9,2048]{2,1,0:T(8,128)S(1)}, s32[8,2048]{1,0:T(8,128)S(1)}, f32[9,4096]{1,0:T(8,128)S(1)}, s32[]{:T(128)}) %tuple.236), condition=%wide.region_7.8_spmd, body=%wide.region_6.7_spmd.sunk | while | flops 914358272 | bytes 417861 | solution.py:39
  249.2 10.4 %fusion.67 = f32[8,9,2048]{2,1,0:T(8,128)S(1)} fusion(f32[8,9,2048]{2,1,0:T(8,128)S(1)} %get-tuple-element.642, s32[]{:T(128)} %get-tuple-element.641, f32[9,4096]{1,0:T(8,128)S(1)} %get-tuple-element.649, s32[2048]{0:T(1024)S(1)} %bitcast.209), kind=kOutput, calls=%fused_computation.14.clone.1 | convolution fusion | flops 914358272 | bytes 401412 | tf_op jit(solution)/shard_map/while/body/eval_jaxpr/dot_general | solution.py:35
  259.6 10.4 %fusion.67 = f32[8,9,2048]{2,1,0:T(8,128)S(1)} fusion(f32[8,9,2048]{2,1,0:T(8,128)S(1)} %get-tuple-element.642, s32[]{:T(128)} %get-tuple-element.641, f32[9,4096]{1,0:T(8,128)S(1)} %get-tuple-element.649, s32[2048]{0:T(1024)S(1)} %bitcast.209), kind=kOutput, calls=%fused_computation.14.clone.1 | convolution fusion | flops 914358272 | bytes 401412 | tf_op jit(solution)/shard_map/while/body/eval_jaxpr/dot_general | solution.py:35
  270.1 10.4 %fusion.67 = f32[8,9,2048]{2,1,0:T(8,128)S(1)} fusion(f32[8,9,2048]{2,1,0:T(8,128)S(1)} %get-tuple-element.642, s32[]{:T(128)} %get-tuple-element.641, f32[9,4096]{1,0:T(8,128)S(1)} %get-tuple-element.649, s32[2048]{0:T(1024)S(1)} %bitcast.209), kind=kOutput, calls=%fused_computation.14.clone.1 | convolution fusion | flops 914358272 | bytes 401412 | tf_op jit(solution)/shard_map/while/body/eval_jaxpr/dot_general | solution.py:35
  280.6 10.4 %fusion.67 = f32[8,9,2048]{2,1,0:T(8,128)S(1)} fusion(f32[8,9,2048]{2,1,0:T(8,128)S(1)} %get-tuple-element.642, s32[]{:T(128)} %get-tuple-element.641, f32[9,4096]{1,0:T(8,128)S(1)} %get-tuple-element.649, s32[2048]{0:T(1024)S(1)} %bitcast.209), kind=kOutput, calls=%fused_computation.14.clone.1 | convolution fusion | flops 914358272 | bytes 401412 | tf_op jit(solution)/shard_map/while/body/eval_jaxpr/dot_general | solution.py:35
  291.0 10.4 %fusion.67 = f32[8,9,2048]{2,1,0:T(8,128)S(1)} fusion(f32[8,9,2048]{2,1,0:T(8,128)S(1)} %get-tuple-element.642, s32[]{:T(128)} %get-tuple-element.641, f32[9,4096]{1,0:T(8,128)S(1)} %get-tuple-element.649, s32[2048]{0:T(1024)S(1)} %bitcast.209), kind=kOutput, calls=%fused_computation.14.clone.1 | convolution fusion | flops 914358272 | bytes 401412 | tf_op jit(solution)/shard_map/while/body/eval_jaxpr/dot_general | solution.py:35
  301.5 10.4 %fusion.67 = f32[8,9,2048]{2,1,0:T(8,128)S(1)} fusion(f32[8,9,2048]{2,1,0:T(8,128)S(1)} %get-tuple-element.642, s32[]{:T(128)} %get-tuple-element.641, f32[9,4096]{1,0:T(8,128)S(1)} %get-tuple-element.649, s32[2048]{0:T(1024)S(1)} %bitcast.209), kind=kOutput, calls=%fused_computation.14.clone.1 | convolution fusion | flops 914358272 | bytes 401412 | tf_op jit(solution)/shard_map/while/body/eval_jaxpr/dot_general | solution.py:35
  311.9 10.4 %fusion.67 = f32[8,9,2048]{2,1,0:T(8,128)S(1)} fusion(f32[8,9,2048]{2,1,0:T(8,128)S(1)} %get-tuple-element.642, s32[]{:T(128)} %get-tuple-element.641, f32[9,4096]{1,0:T(8,128)S(1)} %get-tuple-element.649, s32[2048]{0:T(1024)S(1)} %bitcast.209), kind=kOutput, calls=%fused_computation.14.clone.1 | convolution fusion | flops 914358272 | bytes 401412 | tf_op jit(solution)/shard_map/while/body/eval_jaxpr/dot_general | solution.py:35
  322.4 10.4 %fusion.67 = f32[8,9,2048]{2,1,0:T(8,128)S(1)} fusion(f32[8,9,2048]{2,1,0:T(8,128)S(1)} %get-tuple-element.642, s32[]{:T(128)} %get-tuple-element.641, f32[9,4096]{1,0:T(8,128)S(1)} %get-tuple-element.649, s32[2048]{0:T(1024)S(1)} %bitcast.209), kind=kOutput, calls=%fused_computation.14.clone.1 | convolution fusion | flops 914358272 | bytes 401412 | tf_op jit(solution)/shard_map/while/body/eval_jaxpr/dot_general | solution.py:35
  353.0 25.7 %all-to-all-done.1 = f32[27,128,128]{2,0,1:T(8,128)S(1)} async-done(((f32[27,128,128]{2,0,1:T(8,128)}), f32[27,128,128]{2,0,1:T(8,128)S(1)}, u32[]{:S(2)}, u32[]{:S(2)}) %all-to-all-start.1) | async-done | bytes 1769504 | tf_op jit(solution)/shard_map/all_to_all | solution.py:212
  382.5 10.7 %while.16 = (s32[]{:T(128)}, f32[27,256]{1,0:T(8,128)S(1)}, f32[8,27,2048]{2,0,1:T(8,128)S(1)}, s32[8,2048]{1,0:T(8,128)S(1)}, s32[]{:T(128)}, /*index=5*/s32[]{:T(128)}) while((s32[]{:T(128)}, f32[27,256]{1,0:T(8,128)S(1)}, f32[8,27,2048]{2,0,1:T(8,128)S(1)}, s32[8,2048]{1,0:T(8,128)S(1)}, s32[]{:T(128)}, ...), condition=%wide.region_9.10_spmd.clone, body=%wide.region_8.9_spmd.clone.sunk | while | flops 170407424 | bytes 743511 | solution.py:64
  400.3 13.7 %all-to-all-done.2 = f32[6,128,16]{2,0,1:T(8,128)S(1)} async-done(((f32[6,128,16]{2,0,1:T(8,128)}), f32[6,128,16]{2,0,1:T(8,128)S(1)}, u32[]{:S(2)}, u32[]{:S(2)}) %all-to-all-start.2) | async-done | bytes 49184 | tf_op jit(solution)/shard_map/all_to_all | solution.py:257
  435.1 13.7 %all-to-all-done.3 = f32[6,128,16]{2,0,1:T(8,128)S(1)} async-done(((f32[6,128,16]{2,0,1:T(8,128)}), f32[6,128,16]{2,0,1:T(8,128)S(1)}, u32[]{:S(2)}, u32[]{:S(2)}) %all-to-all-start.3) | async-done | bytes 49184 | tf_op jit(solution)/shard_map/all_to_all | solution.py:266
  522.9 13.8 %all-to-all-done.4 = f32[6,128,16]{2,0,1:T(8,128)S(1)} async-done(((f32[6,128,16]{2,0,1:T(8,128)}), f32[6,128,16]{2,0,1:T(8,128)S(1)}, u32[]{:S(2)}, u32[]{:S(2)}) %all-to-all-start.4) | async-done | bytes 49184 | tf_op jit(solution)/shard_map/all_to_all | solution.py:257
  557.7 13.7 %all-to-all-done.5 = f32[6,128,16]{2,0,1:T(8,128)S(1)} async-done(((f32[6,128,16]{2,0,1:T(8,128)}), f32[6,128,16]{2,0,1:T(8,128)S(1)}, u32[]{:S(2)}, u32[]{:S(2)}) %all-to-all-start.5) | async-done | bytes 49184 | tf_op jit(solution)/shard_map/all_to_all | solution.py:266
  (261 shorter events, 250.6 us)
Async XLA Ops:
  11.1 0.9 copy-start.3
  12.1 13.5 %copy-start.4 = (s32[1,128,128]{2,1,0:T(8,128)S(1)}, s32[1,128,128]{2,1,0:T(8,128)}, u32[]{:S(2)}) copy-start(s32[1,128,128]{2,1,0:T(8,128)} %param.23) | copy-start | bytes 196612
  12.1 13.5 %copy-start.8 = (f32[3,4096]{1,0:T(4,128)S(1)}, f32[3,4096]{1,0:T(4,128)}, u32[]{:S(2)}) copy-start(f32[3,4096]{1,0:T(4,128)} %param.20) | copy-start | bytes 147460
  13.6 98.8 %all-to-all-start = ((f32[14,128,128]{2,0,1:T(8,128)}), f32[14,128,128]{2,0,1:T(8,128)S(1)}, u32[]{:S(2)}, u32[]{:S(2)}) async-start(f32[14,128,128]{2,0,1:T(8,128)} %copy.139), calls=%async_computation | async-start | bytes 2097152 | tf_op jit(solution)/shard_map/all_to_all | solution.py:208
  25.6 85.4 %copy-start.1 = (s32[1,128]{1,0:T(1,128)S(1)}, s32[1,128]{1,0:T(1,128)}, u32[]{:S(2)}) copy-start(s32[1,128]{1,0:T(1,128)} %param.24) | copy-start | bytes 1540
  115.7 5.2 copy-start
  249.0 84.5 %copy-start.2 = (s32[1,128]{1,0:T(1,128)S(1)}, s32[1,128]{1,0:T(1,128)}, u32[]{:S(2)}) copy-start(s32[1,128]{1,0:T(1,128)} %param.24) | copy-start | bytes 1540
  338.4 9.8 %copy-start.6 = (s32[1,128,16]{1,2,0:T(8,128)S(1)}, s32[1,128,16]{1,2,0:T(8,128)}, u32[]{:S(2)}) copy-start(s32[1,128,16]{1,2,0:T(8,128)} %param.25) | copy-start | bytes 24580
  338.4 10.0 %copy-start.7 = (s32[8,256]{1,0:T(8,128)S(1)}, s32[8,256]{1,0:T(8,128)}, u32[]{:S(2)}) copy-start(s32[8,256]{1,0:T(8,128)} %param.26) | copy-start | bytes 24580
  338.4 40.3 %all-to-all-start.1 = ((f32[27,128,128]{2,0,1:T(8,128)}), f32[27,128,128]{2,0,1:T(8,128)S(1)}, u32[]{:S(2)}, u32[]{:S(2)}) async-start(f32[27,128,128]{2,0,1:T(8,128)} %copy.157), calls=%async_computation.1 | async-start | bytes 4194304 | tf_op jit(solution)/shard_map/all_to_all | solution.py:212
  394.3 20.0 %copy-start.5 = (f32[8,256]{1,0:T(8,128)S(1)}, f32[8,256]{1,0:T(8,128)}, u32[]{:S(2)}) copy-start(f32[8,256]{1,0:T(8,128)} %param.27) | copy-start | bytes 24580
  395.3 18.6 %all-to-all-start.2 = ((f32[6,128,16]{2,0,1:T(8,128)}), f32[6,128,16]{2,0,1:T(8,128)S(1)}, u32[]{:S(2)}, u32[]{:S(2)}) async-start(f32[6,128,16]{2,0,1:T(8,128)} %copy.161), calls=%async_computation.2 | async-start | bytes 1048576 | tf_op jit(solution)/shard_map/all_to_all | solution.py:257
  430.6 18.2 %all-to-all-start.3 = ((f32[6,128,16]{2,0,1:T(8,128)}), f32[6,128,16]{2,0,1:T(8,128)S(1)}, u32[]{:S(2)}, u32[]{:S(2)}) async-start(f32[6,128,16]{2,0,1:T(8,128)} %copy.163), calls=%async_computation.3 | async-start | bytes 1048576 | tf_op jit(solution)/shard_map/all_to_all | solution.py:266
  518.8 17.8 %all-to-all-start.4 = ((f32[6,128,16]{2,0,1:T(8,128)}), f32[6,128,16]{2,0,1:T(8,128)S(1)}, u32[]{:S(2)}, u32[]{:S(2)}) async-start(f32[6,128,16]{2,0,1:T(8,128)} %copy.165), calls=%async_computation.4 | async-start | bytes 1048576 | tf_op jit(solution)/shard_map/all_to_all | solution.py:257
  553.2 18.2 %all-to-all-start.5 = ((f32[6,128,16]{2,0,1:T(8,128)}), f32[6,128,16]{2,0,1:T(8,128)S(1)}, u32[]{:S(2)}, u32[]{:S(2)}) async-start(f32[6,128,16]{2,0,1:T(8,128)} %copy.167), calls=%async_computation.5 | async-start | bytes 1048576 | tf_op jit(solution)/shard_map/all_to_all | solution.py:266
where the time goes:
time: 611 us; the launch traced here: 607 us
  matrix products  333 us (55%)
  blocking collectives  94 us (15%)
  waiting for transfers between devices  80.5 us (13%)
  starting transfers between devices  39.5 us (6%)
  local copies, waits for them, and re-layouts  33.2 us (5%)
  other arithmetic  18.8 us (3%)
    dot_general x28, matrix products, select(): jnp.dot(table, onehot, precision=lax.Precision.HIGHEST, preferred_element...  190 us
    dot_general x20, matrix products, accumulate(): lax.dot_general(piece, onehot, (((1,), (1,)), ((), ())), precision=lax.Pr...  144 us
    psum x12, blocking collectives, over_axes(): array = lax.psum(array, axis)  94 us
    all_to_all x2, waiting for transfers between devices, per_device(): lax.all_to_all(outgoing, GX_GY, split_axis=1, concat_axis=1, tiled=True)  27.4 us
    all_to_all x2, waiting for transfers between devices, per_device(): lax.all_to_all(slot_sums, GX_GY, split_axis=1, concat_axis=1, tiled=True)  27.4 us
    all_to_all x1, waiting for transfers between devices, send_results(): lax.all_to_all(payload, GX_GY, split_axis=1, concat_axis=1, tiled=True)  25.7 us
  transfers between devices with their start and end apart: 6, of which 5 were waited for; matrix products, arithmetic and copies ran while one was open for 15% of the time, Pallas kernels for 0%

commit v1 on v0

v1 whole, which is shorter than its diff:
```python
import functools

import jax
import jax.numpy as jnp
from jax import lax
from jax.experimental import pallas as pl
from jax.experimental.pallas import tpu as pltpu
from jax.sharding import PartitionSpec as P

AXES = ("gx", "gy")
DAMPING = 1.0
SYMMETRIC_PAIRS = [(a, b) for a in range(6) for b in range(a, 6)]
LOOKUP = {}
for _place, (_a, _b) in enumerate(SYMMETRIC_PAIRS):
    LOOKUP[_a, _b] = _place
    LOOKUP[_b, _a] = _place
POINT_PAIRS = [(0, 0), (0, 1), (0, 2), (1, 1), (1, 2), (2, 2)]
PARTS = 3

F32 = jnp.float32
BF16 = jnp.bfloat16


def call(kernel, name, out_shape, scratch=(), flops=1_000_000, bytes_accessed=1_000_000):
    return pl.pallas_call(
        kernel,
        out_shape=out_shape,
        scratch_shapes=list(scratch),
        name=name,
        compiler_params=pltpu.CompilerParams(vmem_limit_bytes=48 * 1024 * 1024),
        cost_estimate=pl.CostEstimate(
            flops=flops, bytes_accessed=bytes_accessed, transcendentals=0
        ),
    )


def array(*shape):
    return jax.ShapeDtypeStruct(shape, F32)


def take(table, index):
    return jnp.take_along_axis(table, index, axis=1, mode="promise_in_bounds")


def spread(row, count):
    return jnp.broadcast_to(row, (count, row.shape[1]))


def parts_of(value):
    parts = []
    for _ in range(PARTS):
        part = value.astype(BF16).astype(F32)
        value = value - part
        parts.append(part)
    return parts


def dot_lanes(left, right):
    return lax.dot_general(left, right, (((1,), (1,)), ((), ())), preferred_element_type=F32)


def total(value):
    return jnp.sum(jnp.sum(value, axis=1, keepdims=True), axis=0, keepdims=True)


def pose_kernel(pose_ref, cam_ref, uv_ref, out_ref, table_ref):
    inverse = 1.0 / pose_ref[0:1, :]
    table_ref[0:3, :] = pose_ref[1:4, :] * inverse
    table_ref[3:6, :] = pose_ref[4:7, :]
    table_ref[6:8, :] = jnp.zeros((2, 256), F32)
    low, high = table_ref[:, 0:128], table_ref[:, 128:256]

    def tile(t, carry):
        base = pl.multiple_of(t * 8, 8)
        index = cam_ref[pl.ds(base, 8), :]
        lane = index & 127
        for i in range(8):
            where = spread(lane[i : i + 1, :], 8)
            upper = spread(index[i : i + 1, :], 8) >= 128
            out_ref[pl.ds(pl.multiple_of(base * 8 + 8 * i, 8), 8), :] = jnp.where(
                upper, take(high, where), take(low, where)
            )
        out_ref[pl.ds(base * 8 + 6, 8, stride=8), :] = uv_ref[0, pl.ds(base, 8), :]
        out_ref[pl.ds(base * 8 + 7, 8, stride=8), :] = uv_ref[1, pl.ds(base, 8), :]
        return carry

    lax.fori_loop(0, 16, tile, 0)


def position_kernel(points_ref, index_ref, out_ref):
    def group(g, carry):
        base = pl.multiple_of(g * 32, 32)
        index = [index_ref[pl.ds(base + 8 * k, 8), :] for k in range(4)]
        lane = [value & 127 for value in index]
        chunk = [value >> 7 for value in index]
        found = [[jnp.zeros((8, 128), F32) for _ in range(4)] for _ in range(3)]
        for h in range(32):
            for r in range(3):
                row = spread(points_ref[r : r + 1, h * 128 : (h + 1) * 128], 8)
                for k in range(4):
                    found[r][k] = jnp.where(chunk[k] == h, take(row, lane[k]), found[r][k])
        for r in range(3):
            for k in range(4):
                out_ref[r, pl.ds(base + 8 * k, 8), :] = found[r][k]
        return carry

    lax.fori_loop(0, 4, group, 0)


def onehot_rows(rows_ref, row, count, where, iota):
    value = spread(row, 16).astype(BF16)
    one, zero = jnp.ones((), BF16), jnp.zeros((), BF16)
    for q in range(count // 16):
        rows_ref[q * 16 : (q + 1) * 16, where : where + 128] = jnp.where(
            iota[q * 16 : (q + 1) * 16] == value, one, zero
        )


def iota_bf16(count):
    return lax.broadcasted_iota(jnp.int32, (count, 128), 0).astype(F32).astype(BF16)


def eliminate_kernel(
    recv_ref, position_ref, index_ref, count_ref, out_ref, term_ref, keep_ref, left_ref, hot_ref,
    sum_ref, table_ref,
):
    live_count = jnp.transpose(spread(count_ref[0:1, :], 128))
    keep_ref[11, :, :] = jnp.where(
        lax.broadcasted_iota(jnp.int32, (128, 128), 1) < live_count, 1.0, 0.0
    )

    def prepare(t, carry):
        base = pl.multiple_of(t * 8, 8)
        row = [recv_ref[pl.ds(base * 8 + r, 8, stride=8), :] for r in range(8)]
        x = [position_ref[r, pl.ds(base, 8), :] for r in range(3)]
        live = keep_ref[11, pl.ds(base, 8), :]
        q1, q2, q3 = row[0], row[1], row[2]
        s1, s2, s3 = q1 * q1, q2 * q2, q3 * q3
        scale = 1.0 / (1.0 + s1 + s2 + s3)
        q12, q13, q23 = q1 * q2, q1 * q3, q2 * q3
        rot = [
            (1.0 + s1 - s2 - s3) * scale,
            2.0 * (q12 - q3) * scale,
            2.0 * (q13 + q2) * scale,
            2.0 * (q12 + q3) * scale,
            (1.0 - s1 + s2 - s3) * scale,
            2.0 * (q23 - q1) * scale,
            2.0 * (q13 - q2) * scale,
            2.0 * (q23 + q1) * scale,
            (1.0 - s1 - s2 + s3) * scale,
        ]
        cam = [
            rot[3 * a] * x[0] + rot[3 * a + 1] * x[1] + rot[3 * a + 2] * x[2] + row[3 + a]
            for a in range(3)
        ]
        inverse = 1.0 / cam[2]
        u, v = cam[0] * inverse, cam[1] * inverse
        residue = [(u - row[6]) * live, (v - row[7]) * live]
        scaled = inverse * live
        jac = [
            [scaled * (rot[k] - u * rot[6 + k]) for k in range(3)],
            [scaled * (rot[3 + k] - v * rot[6 + k]) for k in range(3)],
        ]
        terms = [jac[0][k] * jac[0][l] + jac[1][k] * jac[1][l] for k, l in POINT_PAIRS]
        terms += [jac[0][k] * residue[0] + jac[1][k] * residue[1] for k in range(3)]
        for r in range(9):
            term_ref[r, pl.ds(base, 8), :] = terms[r]
        for r, value in enumerate(jac[0] + jac[1] + residue + [u, v, inverse]):
            keep_ref[r, pl.ds(base, 8), :] = value
        return carry

    lax.fori_loop(0, 16, prepare, 0)

    iota_chunk, iota_lane = iota_bf16(16), iota_bf16(256)
    zero = jnp.zeros((), BF16)
    sum_ref[...] = jnp.zeros_like(sum_ref)

    def build(t, side):
        base = pl.multiple_of(t * 8, 8)
        index = index_ref[pl.ds(base, 8), :]
        lane, chunk = (index & 255).astype(F32), (index >> 8).astype(F32)
        masks = []
        for i in range(8):
            onehot_rows(hot_ref.at[side], lane[i : i + 1, :], 256, i * 128, iota_lane)
            masks.append(iota_chunk == spread(chunk[i : i + 1, :], 16).astype(BF16))
        for r in range(9):
            for n, part in enumerate(parts_of(term_ref[r, pl.ds(base, 8), :])):
                at = (n * 9 + r) * 16
                for i in range(8):
                    left_ref[side, at : at + 16, i * 128 : (i + 1) * 128] = jnp.where(
                        masks[i], spread(part[i : i + 1, :], 16).astype(BF16), zero
                    )

    def product(side):
        sum_ref[...] += dot_lanes(left_ref[side], hot_ref[side])

    build(0, 0)

    def pair(t, carry):
        build(2 * t + 1, 1)
        product(0)
        build(jnp.minimum(2 * t + 2, 15), 0)
        product(1)
        return carry

    lax.fori_loop(0, 8, pair, 0)

    sums = []
    for r in range(9):
        value = sum_ref[r * 16 : (r + 1) * 16, :]
        for n in range(1, PARTS):
            value = value + sum_ref[(n * 9 + r) * 16 : (n * 9 + r + 1) * 16, :]
        sums.append(value)
    hess = [sums[0] + DAMPING, sums[1], sums[2], sums[3] + DAMPING, sums[4], sums[5] + DAMPING]
    cofactor = [
        hess[3] * hess[5] - hess[4] * hess[4],
        hess[2] * hess[4] - hess[1] * hess[5],
        hess[1] * hess[4] - hess[2] * hess[3],
        hess[0] * hess[5] - hess[2] * hess[2],
        hess[1] * hess[2] - hess[0] * hess[4],
        hess[0] * hess[3] - hess[1] * hess[1],
    ]
    determinant = hess[0] * cofactor[0] + hess[1] * cofactor[1] + hess[2] * cofactor[2]
    inv = [value / determinant for value in cofactor]
    grad = sums[6:9]
    solved = [
        inv[0] * grad[0] + inv[1] * grad[1] + inv[2] * grad[2],
        inv[1] * grad[0] + inv[3] * grad[1] + inv[4] * grad[2],
        inv[2] * grad[0] + inv[4] * grad[1] + inv[5] * grad[2],
    ]
    for r, value in enumerate(inv + solved):
        table_ref[r * 16 : (r + 1) * 16, :] = value

    def group(g, carry):
        base = pl.multiple_of(g * 16, 16)
        index = [index_ref[pl.ds(base + 8 * k, 8), :] for k in range(2)]
        lane = [value & 127 for value in index]
        chunk = [value >> 7 for value in index]
        found = [[jnp.zeros((8, 128), F32) for _ in range(9)] for _ in range(2)]
        for h in range(32):
            half = (h % 2) * 128
            for r in range(9):
                at = r * 16 + h // 2
                row = spread(table_ref[at : at + 1, half : half + 128], 8)
                for k in range(2):
                    found[k][r] = jnp.where(chunk[k] == h, take(row, lane[k]), found[k][r])
        for k in range(2):
            here = pl.multiple_of(base + 8 * k, 8)
            kept = [keep_ref[r, pl.ds(here, 8), :] for r in range(12)]
            i0, i1, i2, i3, i4, i5, g0, g1, g2 = found[k]
            p, q = kept[0:3], kept[3:6]
            pv = [
                i0 * p[0] + i1 * p[1] + i2 * p[2],
                i1 * p[0] + i3 * p[1] + i4 * p[2],
                i2 * p[0] + i4 * p[1] + i5 * p[2],
            ]
            qv = [
                i0 * q[0] + i1 * q[1] + i2 * q[2],
                i1 * q[0] + i3 * q[1] + i4 * q[2],
                i2 * q[0] + i4 * q[1] + i5 * q[2],
            ]
            live = kept[11]
            values = [
                kept[8],
                kept[9],
                kept[10],
                live - (pv[0] * p[0] + pv[1] * p[1] + pv[2] * p[2]),
                -(pv[0] * q[0] + pv[1] * q[1] + pv[2] * q[2]),
                live - (qv[0] * q[0] + qv[1] * q[1] + qv[2] * q[2]),
                kept[6] - (p[0] * g0 + p[1] * g1 + p[2] * g2),
                kept[7] - (q[0] * g0 + q[1] * g1 + q[2] * g2),
            ]
            for r, value in enumerate(values):
                out_ref[pl.ds(here * 8 + r, 8, stride=8), :] = value
        return carry

    lax.fori_loop(0, 8, group, 0)


def exchange_out(vector_ref, slots_ref, edge_ref, weight_ref, out_ref, turn_ref, left_ref, hot_ref):
    low, high = vector_ref[:, 0:128], vector_ref[:, 128:256]
    for j in range(16):
        index = spread(slots_ref[j : j + 1, :], 8)
        lane = index & 127
        turn_ref[8 * j : 8 * j + 8, :] = jnp.where(index >= 128, take(high, lane), take(low, lane))
    out_ref[:, 0:128] = jnp.transpose(turn_ref[...])
    iota = iota_bf16(128)
    for k in range(8):
        for h in range(2):
            where = (2 * k + h) * 128
            edge = edge_ref[k : k + 1, h * 128 : (h + 1) * 128]
            onehot_rows(hot_ref, (edge >> 4).astype(F32), 128, where, iota)
            slot = spread(edge & 15, 8)
            weight = spread(weight_ref[k : k + 1, h * 128 : (h + 1) * 128], 8)
            for n, part in enumerate(parts_of(weight * (low, high)[h])):
                for j in range(0, 16, 2):
                    both = jnp.concatenate(
                        [jnp.where(slot == j, part, 0.0), jnp.where(slot == j + 1, part, 0.0)], 0
                    )
                    left_ref[n, 8 * j : 8 * j + 16, where : where + 128] = both.astype(BF16)
    summed = dot_lanes(hot_ref[...], left_ref[0])
    for n in range(1, PARTS):
        summed = summed + dot_lanes(hot_ref[...], left_ref[n])
    out_ref[:, 128:256] = summed


def exchange_in(recv_ref, slots_ref, edge_ref, weight_ref, turn_ref, few_ref, cams_ref, near_ref):
    turn_ref[...] = jnp.transpose(recv_ref[:, 0:128])
    for h in range(2):
        sums = jnp.zeros((8, 128), F32)
        for k in range(8):
            edge = edge_ref[k : k + 1, h * 128 : (h + 1) * 128]
            slot, peer = spread(edge & 15, 8), spread(edge >> 4, 8)
            near = jnp.zeros((8, 128), F32)
            for j in range(16):
                near = jnp.where(slot == j, take(turn_ref[8 * j : 8 * j + 8, :], peer), near)
            sums = sums + spread(weight_ref[k : k + 1, h * 128 : (h + 1) * 128], 8) * near
        near_ref[:, h * 128 : (h + 1) * 128] = sums
    scalar = jnp.sum(turn_ref[7:8, :], axis=1, keepdims=True)
    turn_ref[...] = jnp.transpose(recv_ref[:, 128:256])
    iota = iota_bf16(256)
    for j in range(16):
        parts = parts_of(turn_ref[8 * j : 8 * j + 8, :])
        parts += [jnp.zeros((8, 128), F32)] * (4 - PARTS)
        few_ref[:, j * 128 : (j + 1) * 128] = jnp.concatenate(parts, 0).astype(BF16)
        onehot_rows(cams_ref, slots_ref[j : j + 1, :].astype(F32), 256, j * 128, iota)
    flow = dot_lanes(few_ref[...], cams_ref[...])
    back = flow[0:8, :]
    for n in range(1, PARTS):
        back = back + flow[8 * n : 8 * n + 8, :]
    return near_ref[...], back, scalar


OUT_SCRATCH = [
    pltpu.VMEM((128, 128), F32),
    pltpu.VMEM((PARTS, 128, 2048), BF16),
    pltpu.VMEM((128, 2048), BF16),
]
IN_SCRATCH = [
    pltpu.VMEM((32, 2048), BF16),
    pltpu.VMEM((256, 2048), BF16),
    pltpu.VMEM((8, 256), F32),
]


def block_product(system_ref, vector):
    return [
        sum(system_ref[LOOKUP[a, b] : LOOKUP[a, b] + 1, :] * vector[b] for b in range(6))
        for a in range(6)
    ]


def camera_kernel(
    recv_ref, index_ref, slots_ref, edge_ref, weight_ref, out_ref, system_ref, vector_ref,
    entry_ref, left_ref, hot_ref, sum_ref, turn_ref, edge_left_ref, edge_hot_ref,
):
    iota = iota_bf16(256)
    sum_ref[...] = jnp.zeros_like(sum_ref)
    entry_ref[27 * 8 : 32 * 8, :] = jnp.zeros((40, 128), F32)

    def build(t, side):
        base = pl.multiple_of(t * 8, 8)
        u, v, w, s00, s01, s11, f0, f1 = [
            recv_ref[pl.ds(base * 8 + r, 8, stride=8), :] for r in range(8)
        ]
        zero = jnp.zeros((8, 128), F32)
        uv = u * v
        top = [-uv, 1.0 + u * u, -v, w, zero, -u * w]
        low = [-1.0 - v * v, uv, u, zero, w, -v * w]
        g = [s00 * top[k] + s01 * low[k] for k in range(6)]
        h = [s01 * top[k] + s11 * low[k] for k in range(6)]
        for r, (a, b) in enumerate(SYMMETRIC_PAIRS):
            entry_ref[8 * r : 8 * r + 8, :] = top[a] * g[b] + low[a] * h[b]
        for a in range(6):
            entry_ref[8 * (21 + a) : 8 * (22 + a), :] = top[a] * f0 + low[a] * f1
        index = index_ref[pl.ds(base, 8), :].astype(F32)
        for i in range(8):
            onehot_rows(hot_ref.at[side], index[i : i + 1, :], 256, i * 128, iota)
            for n, part in enumerate(parts_of(entry_ref[pl.ds(i, 32, stride=8), :])):
                left_ref[side, n * 32 : (n + 1) * 32, i * 128 : (i + 1) * 128] = part.astype(BF16)

    def product(side):
        sum_ref[...] += dot_lanes(left_ref[side], hot_ref[side])

    build(0, 0)

    def pair(t, carry):
        build(2 * t + 1, 1)
        product(0)
        build(jnp.minimum(2 * t + 2, 15), 0)
        product(1)
        return carry

    lax.fori_loop(0, 8, pair, 0)
    summed = sum_ref[0:32, :]
    for n in range(1, PARTS):
        summed = summed + sum_ref[32 * n : 32 * n + 32, :]
    system_ref[0:32, :] = summed
    partial = jnp.zeros((1, 256), F32)
    for a in range(6):
        at = LOOKUP[a, a]
        diagonal = system_ref[at : at + 1, :] + DAMPING
        residual = -system_ref[21 + a : 22 + a, :]
        scaled = residual / diagonal
        partial = partial + residual * scaled
        vector_ref[a : a + 1, :] = scaled
    vector_ref[6:7, :] = jnp.ones((1, 256), F32)
    vector_ref[7:8, :] = jnp.broadcast_to(jnp.sum(partial, axis=1, keepdims=True), (1, 256))
    exchange_out(
        vector_ref, slots_ref, edge_ref, weight_ref, out_ref, turn_ref, edge_left_ref, edge_hot_ref
    )


def operator_rows(system_ref, vector_ref, degree, near, back):
    vector = [vector_ref[a : a + 1, :] for a in range(6)]
    own = block_product(system_ref, vector)
    return [
        own[a] + (DAMPING + degree) * vector[a] - near[a : a + 1, :] - back[a : a + 1, :]
        for a in range(6)
    ]


def first_kernel(
    recv_ref, system_ref, vector_ref, slots_ref, edge_ref, weight_ref, out_ref, image_ref, next_ref,
    turn_ref, left_ref, hot_ref, few_ref, cams_ref, near_ref,
):
    near, back, scalar = exchange_in(
        recv_ref, slots_ref, edge_ref, weight_ref, turn_ref, few_ref, cams_ref, near_ref
    )
    degree = jnp.sum(weight_ref[...], axis=0, keepdims=True) + back[6:7, :]
    image = operator_rows(system_ref, vector_ref, degree, near, back)
    partial = jnp.zeros((1, 256), F32)
    for a in range(6):
        at = LOOKUP[a, a]
        partial = partial + vector_ref[a : a + 1, :] * image[a]
        image_ref[a : a + 1, :] = image[a]
        next_ref[a : a + 1, :] = image[a] / (system_ref[at : at + 1, :] + DAMPING)
    image_ref[6:7, :] = degree
    image_ref[7:8, :] = jnp.broadcast_to(scalar, (1, 256))
    next_ref[6:7, :] = jnp.ones((1, 256), F32)
    next_ref[7:8, :] = jnp.broadcast_to(jnp.sum(partial, axis=1, keepdims=True), (1, 256))
    exchange_out(
        next_ref, slots_ref, edge_ref, weight_ref, out_ref, turn_ref, left_ref, hot_ref
    )


def second_kernel(
    recv_ref, system_ref, vector_ref, image_ref, next_ref, slots_ref, edge_ref, weight_ref,
    out_ref, state_ref, turn_ref, few_ref, cams_ref, near_ref,
):
    near, back, curvature = exchange_in(
        recv_ref, slots_ref, edge_ref, weight_ref, turn_ref, few_ref, cams_ref, near_ref
    )
    degree = image_ref[6:7, :]
    alpha = image_ref[7:8, :] / curvature
    image_next = operator_rows(system_ref, next_ref, degree, near, back)
    sums = [jnp.zeros((1, 256), F32) for _ in range(3)]
    for a in range(6):
        at = LOOKUP[a, a]
        vector, image = vector_ref[a : a + 1, :], image_ref[a : a + 1, :]
        residual = -system_ref[21 + a : 22 + a, :] - alpha * image
        scaled = residual / (system_ref[at : at + 1, :] + DAMPING)
        scaled_image = image - alpha * image_next[a]
        sums[0] = sums[0] + residual * scaled
        sums[1] = sums[1] + scaled * scaled_image
        sums[2] = sums[2] + scaled * image + vector * scaled_image
        state_ref[a : a + 1, :] = residual
        state_ref[8 + a : 9 + a, :] = scaled
        state_ref[16 + a : 17 + a, :] = scaled_image
    state_ref[6:7, :] = alpha
    state_ref[7:8, :] = jnp.broadcast_to(curvature, (1, 256))
    lane = lax.broadcasted_iota(jnp.int32, (128, 128), 1)
    rows = [jnp.sum(value, axis=1, keepdims=True) for value in sums]
    out_ref[...] = jnp.where(lane == 0, rows[0], jnp.where(lane == 1, rows[1], rows[2]))


def last_kernel(recv_ref, vector_ref, image_ref, state_ref, step_ref, residual_ref):
    sums = jnp.sum(recv_ref[...], axis=0, keepdims=True)
    fresh, inner, cross = sums[:, 0:1], sums[:, 1:2], sums[:, 2:3]
    alpha, curvature = state_ref[6:7, 0:1], state_ref[7:8, 0:1]
    beta = fresh / image_ref[7:8, 0:1]
    alpha_next = fresh / (inner + beta * cross + beta * beta * curvature)
    vector, image = vector_ref[0:6, :], image_ref[0:6, :]
    direction = state_ref[8:14, :] + beta * vector
    step_ref[...] = alpha * vector + alpha_next * direction
    residual_ref[...] = state_ref[0:6, :] - alpha_next * (state_ref[16:22, :] + beta * image)


def swap(payload):
    return lax.all_to_all(payload, AXES, split_axis=0, concat_axis=0, tiled=True)


def per_device(
    cam_pose, points, obs_uv, obs_cam, obs_pt, block_count, send_list, edge_slot, edge_weight
):
    cam_index = obs_cam.reshape(128, 128)
    point_index = obs_pt.reshape(128, 128)
    slots = jnp.transpose(send_list.reshape(128, 16))
    poses = call(pose_kernel, "poses", array(1024, 128), [pltpu.VMEM((8, 256), F32)])(
        cam_pose, cam_index, obs_uv.reshape(2, 128, 128)
    )
    arrived = swap(poses.reshape(128, 8, 128)).reshape(1024, 128)
    position = call(position_kernel, "positions", array(3, 128, 128))(points, point_index)
    reduced = call(
        eliminate_kernel,
        "eliminate",
        array(1024, 128),
        [
            pltpu.VMEM((9, 128, 128), F32),
            pltpu.VMEM((12, 128, 128), F32),
            pltpu.VMEM((2, 144 * PARTS, 1024), BF16),
            pltpu.VMEM((2, 256, 1024), BF16),
            pltpu.VMEM((144 * PARTS, 256), F32),
            pltpu.VMEM((144, 256), F32),
        ],
    )(arrived, position, point_index, block_count)
    returned = swap(reduced.reshape(128, 8, 128)).reshape(1024, 128)
    payload, system, vector = call(
        camera_kernel,
        "cameras",
        (array(128, 256), array(32, 256), array(8, 256)),
        [
            pltpu.VMEM((256, 128), F32),
            pltpu.VMEM((2, 32 * PARTS, 1024), BF16),
            pltpu.VMEM((2, 256, 1024), BF16),
            pltpu.VMEM((32 * PARTS, 256), F32),
        ]
        + OUT_SCRATCH,
    )(returned, cam_index, slots, edge_slot, edge_weight)
    payload, image, following = call(
        first_kernel,
        "first_product",
        (array(128, 256), array(8, 256), array(8, 256)),
        OUT_SCRATCH + IN_SCRATCH,
    )(swap(payload), system, vector, slots, edge_slot, edge_weight)
    payload, state = call(
        second_kernel,
        "second_product",
        (array(128, 128), array(24, 256)),
        [OUT_SCRATCH[0]] + IN_SCRATCH,
    )(swap(payload), system, vector, image, following, slots, edge_slot, edge_weight)
    return call(last_kernel, "last", (array(6, 256), array(6, 256)))(
        swap(payload.reshape(128, 1, 128)).reshape(128, 128), vector, image, state
    )


def solution(mesh):
    in_specs = (
        P(None, AXES),
        P(None, AXES),
        P(None, AXES, None, None),
        P(AXES, None, None),
        P(AXES, None, None),
        P(AXES, None),
        P(AXES, None, None),
        P(None, AXES),
        P(None, AXES),
    )
    out_specs = (P(None, AXES), P(None, AXES))
    return jax.shard_map(
        per_device, mesh=mesh, in_specs=in_specs, out_specs=out_specs, check_vma=False
    )
```

time: 611 us -> 115 us (0.19)
  matrix products: 333 us -> 0 us
  waiting for transfers between devices: 80.5 us -> 9.13 us
  blocking collectives: 94 us -> 60.4 us
  local copies, waits for them, and re-layouts: 33.2 us -> 2.77 us
  Pallas kernels: 0 us -> 30.4 us
  starting transfers between devices: 39.5 us -> 11.5 us
  other arithmetic: 18.8 us -> 0 us
    dot_general x48 -> x0, matrix products: 333 us -> none  [the longest x28 190 us: select(): jnp.dot(table, onehot, precision=lax.Precision.HIGHEST, preferred_element...]
    psum x12 -> x0, blocking collectives: 94 us -> none  [over_axes(): array = lax.psum(array, axis)]
    all_to_all x6 -> x1, waiting for transfers between devices: 80.5 us -> 9.13 us  [swap(): lax.all_to_all(payload, AXES, split_axis=0, concat_axis=0, tiled=True)]
    all_to_all x0 -> x4, blocking collectives: none -> 60.4 us  [swap(): lax.all_to_all(payload, AXES, split_axis=0, concat_axis=0, tiled=True)]
    pallas_call x0 -> x7, Pallas kernels: none -> 30.4 us  [the longest x1 14 us: per_device(): call(eliminate_kernel, 'eliminate', array(1024, 128), [pltpu.VMEM((9, 128...]
    all_to_all x6 -> x1, starting transfers between devices: 39.5 us -> 11.5 us  [swap(): lax.all_to_all(payload, AXES, split_axis=0, concat_axis=0, tiled=True)]
    dynamic_slice x56 -> x0, local copies, waits for them, and re-layouts: 10.8 us -> none  [the longest x16 10.3 us: add_columns(): lax.scan(accumulate, jnp.zeros((row_count, table_width), jnp.float32), (p...]
    unnamed x37 -> x0, other arithmetic: 8.95 us -> none
  transfers between devices with their start and end apart: 6 -> 1, of which waited for: 5 -> 1; matrix products, arithmetic and copies ran while one was open for 15% -> 0% of each run, Pallas kernels for 0% -> 4%
where the time goes in v1:
time: 115 us
  blocking collectives  60.4 us (53%)
  Pallas kernels  30.4 us (26%)
  starting transfers between devices  11.5 us (10%)
  waiting for transfers between devices  9.13 us (8%)
  local copies, waits for them, and re-layouts  2.77 us (2%)
    all_to_all x4, blocking collectives, swap(): lax.all_to_all(payload, AXES, split_axis=0, concat_axis=0, tiled=True)  60.4 us
    pallas_call x1, Pallas kernels, per_device(): call(eliminate_kernel, 'eliminate', array(1024, 128), [pltpu.VMEM((9, 128...  14 us
    all_to_all x1, starting transfers between devices, swap(): lax.all_to_all(payload, AXES, split_axis=0, concat_axis=0, tiled=True)  11.5 us
    all_to_all x1, waiting for transfers between devices, swap(): lax.all_to_all(payload, AXES, split_axis=0, concat_axis=0, tiled=True)  9.13 us
    pallas_call x1, Pallas kernels, per_device(): call(camera_kernel, 'cameras', (array(128, 256), array(32, 256), array(8,...  5.62 us
    pallas_call x1, Pallas kernels, per_device(): call(position_kernel, 'positions', array(3, 128, 128))(points, point_index)  4.56 us
    pallas_call x1, Pallas kernels, per_device(): call(pose_kernel, 'poses', array(1024, 128), [pltpu.VMEM((8, 256), F32)])  2.52 us
    unnamed x22, local copies, waits for them, and re-layouts  2.49 us
  transfers between devices with their start and end apart: 1, of which 1 were waited for; matrix products, arithmetic and copies ran while one was open for 0% of the time, Pallas kernels for 4%

profile of v1, /device:TPU:1, one launch (start us, length us, event | category | flops | bytes accessed | tf_op | source)
XLA Modules:
  0.0 114.9 jit_solution(5013306992222123952)
XLA Ops:
  0.6 0.0 copy-start.1
  0.6 0.8 copy-done.1
  1.5 0.0 copy-start.3
  1.5 0.9 copy-done.3
  2.4 0.7 copy-done.8
  3.1 2.5 %poses.1 = f32[1024,128]{1,0:T(8,128)} custom-call(f32[7,256]{1,0:T(8,128)S(1)} %copy-done.8, s32[128,128]{1,0:T(8,128)S(1)} %bitcast.29, f32[2,128,128]{2,1,0:T(8,128)S(1)} %bitcast.34), custom_call_target="tpu_custom_call" | custom-call | flops 1000000 | bytes 1000000 | tf_op jit(solution)/shard_map/poses/pallas_call | solution.py:499
  5.6 11.5 %all-to-all-start = ((f32[128,8,128]{2,1,0:T(8,128)}), f32[128,8,128]{2,1,0:T(8,128)S(1)}, u32[]{:S(2)}, u32[]{:S(2)}) async-start(f32[128,8,128]{2,1,0:T(8,128)} %bitcast.2), calls=%async_computation | async-start | bytes 1048576 | tf_op jit(solution)/shard_map/all_to_all | solution.py:490
  17.1 0.0 copy-done
  17.1 0.0 copy-done.7
  17.1 4.6 %positions.1.position_ref = f32[3,128,128]{2,1,0:T(8,128)S(1)} custom-call(f32[3,4096]{1,0:T(4,128)S(1)} %copy-done.7, s32[128,128]{1,0:T(8,128)S(1)} %bitcast.27), custom_call_target="tpu_custom_call" | custom-call | flops 1000000 | bytes 1000000 | tf_op jit(solution)/shard_map/positions/pallas_call | solution.py:503
  21.7 0.0 copy-start.9
  21.7 9.1 %all-to-all-done = f32[128,8,128]{2,1,0:T(8,128)S(1)} async-done(((f32[128,8,128]{2,1,0:T(8,128)}), f32[128,8,128]{2,1,0:T(8,128)S(1)}, u32[]{:S(2)}, u32[]{:S(2)}) %all-to-all-start) | async-done | bytes 524320 | tf_op jit(solution)/shard_map/all_to_all | solution.py:490
  30.8 0.0 copy-done.9
  30.8 14.0 %eliminate.1 = f32[1024,128]{1,0:T(8,128)S(1)} custom-call(f32[1024,128]{1,0:T(8,128)S(1)} %bitcast.22, f32[3,128,128]{2,1,0:T(8,128)S(1)} %positions.1.position_ref, s32[128,128]{1,0:T(8,128)S(1)} %bitcast.28, s32[1,128]{1,0:T(1,128)S(1)} %copy-done.9), custom_call_target="tpu_custom_call" | custom-call | flops 1000000 | bytes 1000000 | tf_op jit(solution)/shard_map/eliminate/pallas_call | solution.py:504
  44.8 0.0 copy-start.2
  44.8 0.0 copy-start.4
  44.9 0.0 copy-start.5
  44.9 0.0 copy-start.6
  44.9 18.0 %all_to_all.37 = f32[128,8,128]{2,1,0:T(8,128)S(1)} all-to-all(f32[128,8,128]{2,1,0:T(8,128)S(1)} %bitcast.23), channel_id=1, replica_groups=mesh['gx'=4,'gy'=32] {'gx','gy'}, dimensions={0} | all-to-all | bytes 1048576 | tf_op jit(solution)/shard_map/all_to_all | solution.py:490
  62.9 0.0 copy-done.2
  62.9 0.0 copy-done.4
  62.9 0.0 copy-done.5
  62.9 0.0 copy-done.6
  62.9 5.6 %cameras.1 = (f32[128,256]{1,0:T(8,128)S(1)}, f32[32,256]{1,0:T(8,128)S(1)}, f32[8,256]{1,0:T(8,128)S(1)}) custom-call(f32[1024,128]{1,0:T(8,128)S(1)} %bitcast.24, s32[128,128]{1,0:T(8,128)S(1)} %bitcast.30, s32[16,128]{1,0:T(8,128)S(1)} %bitcast.35, s32[8,256]{1,0:T(8,128)S(1)} %copy-done.5, f32[8,256]{1,0:T(8,128)S(1)} %copy-done.6), custom_call_target="tpu_custom_call" | custom-call | flops 1000000 | bytes 1000000 | tf_op jit(solution)/shard_map/cameras/pallas_call | solution.py:518
  68.6 0.1 copy.11
  68.7 14.4 %all_to_all.38 = f32[128,1,256]{2,1,0:T(1,128)S(1)} all-to-all(f32[128,1,256]{2,1,0:T(1,128)S(1)} %copy.11), channel_id=1, replica_groups=mesh['gx'=4,'gy'=32] {'gx','gy'}, dimensions={0} | all-to-all | bytes 262144 | tf_op jit(solution)/shard_map/all_to_all | solution.py:490
  83.1 2.0 %first_product.1 = (f32[128,256]{1,0:T(8,128)S(1)}, f32[8,256]{1,0:T(8,128)S(1)}, f32[8,256]{1,0:T(8,128)S(1)}) custom-call(f32[128,256]{1,0:T(8,128)S(1)} %bitcast.26, f32[32,256]{1,0:T(8,128)S(1)} %get-tuple-element.11.system_ref, f32[8,256]{1,0:T(8,128)S(1)} %get-tuple-element.12.vector_ref, s32[16,128]{1,0:T(8,128)S(1)} %bitcast.36, ...), custom_call_target="tpu_custom_call" | custom-call | flops 1000000 | bytes 1000000 | tf_op jit(solution)/shard_map/first_product/pallas_call | solution.py:530
  85.1 0.1 copy.12
  85.3 14.3 %all_to_all.39 = f32[128,1,256]{2,1,0:T(1,128)S(1)} all-to-all(f32[128,1,256]{2,1,0:T(1,128)S(1)} %copy.12), channel_id=1, replica_groups=mesh['gx'=4,'gy'=32] {'gx','gy'}, dimensions={0} | all-to-all | bytes 262144 | tf_op jit(solution)/shard_map/all_to_all | solution.py:490
  99.5 0.8 second_product.1
  100.3 13.7 %all_to_all.40 = f32[128,1,128]{2,1,0:T(1,128)S(1)} all-to-all(f32[128,1,128]{2,1,0:T(1,128)S(1)} %bitcast.38), channel_id=1, replica_groups=mesh['gx'=4,'gy'=32] {'gx','gy'}, dimensions={0} | all-to-all | bytes 131072 | tf_op jit(solution)/shard_map/all_to_all | solution.py:490
  114.0 0.9 last.1
  (5 shorter events, 0.0 us)
Async XLA Ops:
  0.6 0.8 copy-start.1
  1.5 0.9 copy-start.3
  2.4 0.7 copy-start.8
  5.6 11.5 %copy-start = (s32[1,128,128]{2,1,0:T(8,128)S(1)}, s32[1,128,128]{2,1,0:T(8,128)}, u32[]{:S(2)}) copy-start(s32[1,128,128]{2,1,0:T(8,128)} %param.13) | copy-start | bytes 196612
  5.6 11.5 %copy-start.7 = (f32[3,4096]{1,0:T(4,128)S(1)}, f32[3,4096]{1,0:T(4,128)}, u32[]{:S(2)}) copy-start(f32[3,4096]{1,0:T(4,128)} %points_ref.1) | copy-start | bytes 147460
  5.6 25.2 %all-to-all-start = ((f32[128,8,128]{2,1,0:T(8,128)}), f32[128,8,128]{2,1,0:T(8,128)S(1)}, u32[]{:S(2)}, u32[]{:S(2)}) async-start(f32[128,8,128]{2,1,0:T(8,128)} %bitcast.2), calls=%async_computation | async-start | bytes 1048576 | tf_op jit(solution)/shard_map/all_to_all | solution.py:490
  21.7 9.1 %copy-start.9 = (s32[1,128]{1,0:T(1,128)S(1)}, s32[1,128]{1,0:T(1,128)}, u32[]{:S(2)}) copy-start(s32[1,128]{1,0:T(1,128)} %count_ref.1) | copy-start | bytes 1540
  44.8 18.1 %copy-start.2 = (s32[1,128,128]{2,1,0:T(8,128)S(1)}, s32[1,128,128]{2,1,0:T(8,128)}, u32[]{:S(2)}) copy-start(s32[1,128,128]{2,1,0:T(8,128)} %param.12) | copy-start | bytes 196612
  44.8 18.1 %copy-start.4 = (s32[1,128,16]{1,2,0:T(8,128)S(1)}, s32[1,128,16]{1,2,0:T(8,128)}, u32[]{:S(2)}) copy-start(s32[1,128,16]{1,2,0:T(8,128)} %param.15) | copy-start | bytes 24580
  44.9 18.1 %copy-start.5 = (s32[8,256]{1,0:T(8,128)S(1)}, s32[8,256]{1,0:T(8,128)}, u32[]{:S(2)}) copy-start(s32[8,256]{1,0:T(8,128)} %edge_ref.5) | copy-start | bytes 24580
  44.9 18.1 %copy-start.6 = (f32[8,256]{1,0:T(8,128)S(1)}, f32[8,256]{1,0:T(8,128)}, u32[]{:S(2)}) copy-start(f32[8,256]{1,0:T(8,128)} %weight_ref.5) | copy-start | bytes 24580

commit v2 on v1

--- a/solution.py
+++ b/solution.py
@@ -15,16 +15,19 @@
     LOOKUP[_a, _b] = _place
     LOOKUP[_b, _a] = _place
 POINT_PAIRS = [(0, 0), (0, 1), (0, 2), (1, 1), (1, 2), (2, 2)]
-PARTS = 3
+PARTS = 2
 
 F32 = jnp.float32
 BF16 = jnp.bfloat16
 
 
-def call(kernel, name, out_shape, scratch=(), flops=1_000_000, bytes_accessed=1_000_000):
+def call(
+    kernel, name, out_shape, scratch=(), flops=1_000_000, bytes_accessed=1_000_000, **specs
+):
     return pl.pallas_call(
         kernel,
         out_shape=out_shape,
+        **specs,
         scratch_shapes=list(scratch),
         name=name,
         compiler_params=pltpu.CompilerParams(vmem_limit_bytes=48 * 1024 * 1024),
@@ -59,32 +62,37 @@
     return lax.dot_general(left, right, (((1,), (1,)), ((), ())), preferred_element_type=F32)
 
 
-def total(value):
-    return jnp.sum(jnp.sum(value, axis=1, keepdims=True), axis=0, keepdims=True)
-
-
-def pose_kernel(pose_ref, cam_ref, uv_ref, out_ref, table_ref):
+def pose_kernel(
+    pose_hbm, cam_hbm, uv_hbm, out_ref, pose_ref, cam_ref, uv_ref, pose_sem, cam_sem, uv_sem
+):
+    copies = [
+        pltpu.make_async_copy(pose_hbm, pose_ref, pose_sem),
+        pltpu.make_async_copy(cam_hbm, cam_ref, cam_sem),
+        pltpu.make_async_copy(uv_hbm, uv_ref, uv_sem),
+    ]
+    for copy in copies:
+        copy.start()
+    for copy in copies:
+        copy.wait()
     inverse = 1.0 / pose_ref[0:1, :]
-    table_ref[0:3, :] = pose_ref[1:4, :] * inverse
-    table_ref[3:6, :] = pose_ref[4:7, :]
-    table_ref[6:8, :] = jnp.zeros((2, 256), F32)
-    low, high = table_ref[:, 0:128], table_ref[:, 128:256]
+    pose_ref[1:4, :] = pose_ref[1:4, :] * inverse
 
     def tile(t, carry):
         base = pl.multiple_of(t * 8, 8)
         index = cam_ref[pl.ds(base, 8), :]
-        lane = index & 127
-        for i in range(8):
-            where = spread(lane[i : i + 1, :], 8)
-            upper = spread(index[i : i + 1, :], 8) >= 128
-            out_ref[pl.ds(pl.multiple_of(base * 8 + 8 * i, 8), 8), :] = jnp.where(
-                upper, take(high, where), take(low, where)
+        lane, upper = index & 127, index >= 128
+        for r in range(6):
+            row = pose_ref[1 + r : 2 + r, :]
+            out_ref[pl.ds(base * 8 + r, 8, stride=8), :] = jnp.where(
+                upper,
+                take(spread(row[:, 128:256], 8), lane),
+                take(spread(row[:, 0:128], 8), lane),
             )
-        out_ref[pl.ds(base * 8 + 6, 8, stride=8), :] = uv_ref[0, pl.ds(base, 8), :]
-        out_ref[pl.ds(base * 8 + 7, 8, stride=8), :] = uv_ref[1, pl.ds(base, 8), :]
+        for r in range(2):
+            out_ref[pl.ds(base * 8 + 6 + r, 8, stride=8), :] = uv_ref[r, pl.ds(base, 8), :]
         return carry
 
-    lax.fori_loop(0, 16, tile, 0)
+    lax.fori_loop(0, 16, tile, 0, unroll=4)
 
 
 def position_kernel(points_ref, index_ref, out_ref):
@@ -94,10 +102,10 @@
         lane = [value & 127 for value in index]
         chunk = [value >> 7 for value in index]
         found = [[jnp.zeros((8, 128), F32) for _ in range(4)] for _ in range(3)]
-        for h in range(32):
-            for r in range(3):
-                row = spread(points_ref[r : r + 1, h * 128 : (h + 1) * 128], 8)
-                for k in range(4):
+        for k in range(4):
+            for h in range(32):
+                for r in range(3):
+                    row = spread(points_ref[r : r + 1, h * 128 : (h + 1) * 128], 8)
                     found[r][k] = jnp.where(chunk[k] == h, take(row, lane[k]), found[r][k])
         for r in range(3):
             for k in range(4):
@@ -122,7 +130,7 @@
 
 def eliminate_kernel(
     recv_ref, position_ref, index_ref, count_ref, out_ref, term_ref, keep_ref, left_ref, hot_ref,
-    sum_ref, table_ref,
+    sum_ref, half_ref, table_ref, ninth_ref, parts_ref, picked_ref, found_ref,
 ):
     live_count = jnp.transpose(spread(count_ref[0:1, :], 128))
     keep_ref[11, :, :] = jnp.where(
@@ -164,7 +172,7 @@
         terms = [jac[0][k] * jac[0][l] + jac[1][k] * jac[1][l] for k, l in POINT_PAIRS]
         terms += [jac[0][k] * residue[0] + jac[1][k] * residue[1] for k in range(3)]
         for r in range(9):
-            term_ref[r, pl.ds(base, 8), :] = terms[r]
+            term_ref[t, 8 * r : 8 * r + 8, :] = terms[r]
         for r, value in enumerate(jac[0] + jac[1] + residue + [u, v, inverse]):
             keep_ref[r, pl.ds(base, 8), :] = value
         return carry
@@ -173,108 +181,152 @@
 
     iota_chunk, iota_lane = iota_bf16(16), iota_bf16(256)
     zero = jnp.zeros((), BF16)
+
+    def build(t, side, half):
+        index = index_ref[pl.ds(pl.multiple_of(t * 8, 8), 8), :]
+        lane, chunk = (index & 255).astype(F32), (index >> 8).astype(F32)
+        for i in range(8):
+            at = half * 1024 + i * 128
+            onehot_rows(hot_ref.at[t], lane[i : i + 1, :], 256, i * 128, iota_lane)
+            where = spread(chunk[i : i + 1, :], 16).astype(BF16)
+            both = jnp.concatenate(parts_of(term_ref[t, pl.ds(i, 8, stride=8), :]), 0).astype(BF16)
+            for h in range(16):
+                left_ref[side, h * 16 : (h + 1) * 16, at : at + 128] = jnp.where(
+                    where == h, both, zero
+                )
+            mask = iota_chunk == where
+            for n, part in enumerate(parts_of(term_ref[t, 64 + i : 65 + i, :])):
+                left_ref[side, 256 + 16 * n : 272 + 16 * n, at : at + 128] = jnp.where(
+                    mask, spread(part, 16).astype(BF16), zero
+                )
+
+    def build_two(g, side):
+        build(2 * g, side, 0)
+        build(2 * g + 1, side, 1)
+
+    def hot_two(g):
+        return jnp.concatenate([hot_ref[2 * g], hot_ref[2 * g + 1]], 1)
+
+    def product(g, side):
+        sum_ref[...] += dot_lanes(left_ref[side], hot_two(g))
+
     sum_ref[...] = jnp.zeros_like(sum_ref)
-
-    def build(t, side):
+    build_two(0, 0)
+
+    def pair(p, carry):
+        build_two(2 * p + 1, 1)
+        product(2 * p, 0)
+        build_two(2 * p + 2, 0)
+        product(2 * p + 1, 1)
+        return carry
+
+    lax.fori_loop(0, 3, pair, 0)
+    build_two(7, 1)
+    product(6, 0)
+    product(7, 1)
+
+    for side in range(2):
+        lanes = slice(side * 128, side * 128 + 128)
+        half_ref[...] = sum_ref[:, lanes]
+        sums = [
+            half_ref[pl.ds(r, 16, stride=16), :] + half_ref[pl.ds(8 + r, 16, stride=16), :]
+            for r in range(8)
+        ] + [half_ref[256:272, :] + half_ref[272:288, :]]
+        hess = [sums[0] + DAMPING, sums[1], sums[2], sums[3] + DAMPING, sums[4], sums[5] + DAMPING]
+        cofactor = [
+            hess[3] * hess[5] - hess[4] * hess[4],
+            hess[2] * hess[4] - hess[1] * hess[5],
+            hess[1] * hess[4] - hess[2] * hess[3],
+            hess[0] * hess[5] - hess[2] * hess[2],
+            hess[1] * hess[2] - hess[0] * hess[4],
+            hess[0] * hess[3] - hess[1] * hess[1],
+        ]
+        determinant = hess[0] * cofactor[0] + hess[1] * cofactor[1] + hess[2] * cofactor[2]
+        inv = [value / determinant for value in cofactor]
+        grad = sums[6:9]
+        solved = [
+            inv[0] * grad[0] + inv[1] * grad[1] + inv[2] * grad[2],
+            inv[1] * grad[0] + inv[3] * grad[1] + inv[4] * grad[2],
+            inv[2] * grad[0] + inv[4] * grad[1] + inv[5] * grad[2],
+        ]
+        for r, value in enumerate(inv + solved[0:2]):
+            table_ref[pl.ds(r, 16, stride=8), :] = value
+        ninth_ref[:, lanes] = solved[2]
+        for h in range(16):
+            parts_ref[h * 16 : (h + 1) * 16, lanes] = jnp.concatenate(
+                parts_of(table_ref[8 * h : 8 * h + 8, :]), 0
+            ).astype(BF16)
+
+    def pick(g, side):
+        picked_ref[side] = jnp.dot(parts_ref[...], hot_two(g), preferred_element_type=F32)
+
+    def finish(t, side, half):
         base = pl.multiple_of(t * 8, 8)
         index = index_ref[pl.ds(base, 8), :]
-        lane, chunk = (index & 255).astype(F32), (index >> 8).astype(F32)
-        masks = []
+        chunk = index >> 8
         for i in range(8):
-            onehot_rows(hot_ref.at[side], lane[i : i + 1, :], 256, i * 128, iota_lane)
-            masks.append(iota_chunk == spread(chunk[i : i + 1, :], 16).astype(BF16))
-        for r in range(9):
-            for n, part in enumerate(parts_of(term_ref[r, pl.ds(base, 8), :])):
-                at = (n * 9 + r) * 16
-                for i in range(8):
-                    left_ref[side, at : at + 16, i * 128 : (i + 1) * 128] = jnp.where(
-                        masks[i], spread(part[i : i + 1, :], 16).astype(BF16), zero
-                    )
-
-    def product(side):
-        sum_ref[...] += dot_lanes(left_ref[side], hot_ref[side])
-
-    build(0, 0)
-
-    def pair(t, carry):
-        build(2 * t + 1, 1)
-        product(0)
-        build(jnp.minimum(2 * t + 2, 15), 0)
-        product(1)
+            at = half * 1024 + i * 128
+            where = spread(chunk[i : i + 1, :], 8)
+            first, second = jnp.zeros((8, 128), F32), jnp.zeros((8, 128), F32)
+            for h in range(16):
+                first = jnp.where(
+                    where == h, picked_ref[side, 16 * h : 16 * h + 8, at : at + 128], first
+                )
+                second = jnp.where(
+                    where == h, picked_ref[side, 16 * h + 8 : 16 * h + 16, at : at + 128], second
+                )
+            found_ref[half, 8 * i : 8 * i + 8, :] = first + second
+        lane, chunk = index & 127, index >> 7
+        g2 = jnp.zeros((8, 128), F32)
+        for h in range(32):
+            row = ninth_ref[h // 2 : h // 2 + 1, (h % 2) * 128 : (h % 2) * 128 + 128]
+            g2 = jnp.where(chunk == h, take(spread(row, 8), lane), g2)
+        i0, i1, i2, i3, i4, i5, g0, g1 = [
+            found_ref[half, pl.ds(r, 8, stride=8), :] for r in range(8)
+        ]
+        kept = [keep_ref[r, pl.ds(base, 8), :] for r in range(12)]
+        p, q = kept[0:3], kept[3:6]
+        pv = [
+            i0 * p[0] + i1 * p[1] + i2 * p[2],
+            i1 * p[0] + i3 * p[1] + i4 * p[2],
+            i2 * p[0] + i4 * p[1] + i5 * p[2],
+        ]
+        qv = [
+            i0 * q[0] + i1 * q[1] + i2 * q[2],
+            i1 * q[0] + i3 * q[1] + i4 * q[2],
+            i2 * q[0] + i4 * q[1] + i5 * q[2],
+        ]
+        live = kept[11]
+        values = [
+            kept[8],
+            kept[9],
+            kept[10],
+            live - (pv[0] * p[0] + pv[1] * p[1] + pv[2] * p[2]),
+            -(pv[0] * q[0] + pv[1] * q[1] + pv[2] * q[2]),
+            live - (qv[0] * q[0] + qv[1] * q[1] + qv[2] * q[2]),
+            kept[6] - (p[0] * g0 + p[1] * g1 + p[2] * g2),
+            kept[7] - (q[0] * g0 + q[1] * g1 + q[2] * g2),
+        ]
+        for r, value in enumerate(values):
+            out_ref[pl.ds(base * 8 + r, 8, stride=8), :] = value
+
+    def finish_two(g, side):
+        finish(2 * g, side, 0)
+        finish(2 * g + 1, side, 1)
+
+    pick(0, 0)
+
+    def pick_pair(p, carry):
+        pick(2 * p + 1, 1)
+        finish_two(2 * p, 0)
+        pick(2 * p + 2, 0)
+        finish_two(2 * p + 1, 1)
         return carry
 
-    lax.fori_loop(0, 8, pair, 0)
-
-    sums = []
-    for r in range(9):
-        value = sum_ref[r * 16 : (r + 1) * 16, :]
-        for n in range(1, PARTS):
-            value = value + sum_ref[(n * 9 + r) * 16 : (n * 9 + r + 1) * 16, :]
-        sums.append(value)
-    hess = [sums[0] + DAMPING, sums[1], sums[2], sums[3] + DAMPING, sums[4], sums[5] + DAMPING]
-    cofactor = [
-        hess[3] * hess[5] - hess[4] * hess[4],
-        hess[2] * hess[4] - hess[1] * hess[5],
-        hess[1] * hess[4] - hess[2] * hess[3],
-        hess[0] * hess[5] - hess[2] * hess[2],
-        hess[1] * hess[2] - hess[0] * hess[4],
-        hess[0] * hess[3] - hess[1] * hess[1],
-    ]
-    determinant = hess[0] * cofactor[0] + hess[1] * cofactor[1] + hess[2] * cofactor[2]
-    inv = [value / determinant for value in cofactor]
-    grad = sums[6:9]
-    solved = [
-        inv[0] * grad[0] + inv[1] * grad[1] + inv[2] * grad[2],
-        inv[1] * grad[0] + inv[3] * grad[1] + inv[4] * grad[2],
-        inv[2] * grad[0] + inv[4] * grad[1] + inv[5] * grad[2],
-    ]
-    for r, value in enumerate(inv + solved):
-        table_ref[r * 16 : (r + 1) * 16, :] = value
-
-    def group(g, carry):
-        base = pl.multiple_of(g * 16, 16)
-        index = [index_ref[pl.ds(base + 8 * k, 8), :] for k in range(2)]
-        lane = [value & 127 for value in index]
-        chunk = [value >> 7 for value in index]
-        found = [[jnp.zeros((8, 128), F32) for _ in range(9)] for _ in range(2)]
-        for h in range(32):
-            half = (h % 2) * 128
-            for r in range(9):
-                at = r * 16 + h // 2
-                row = spread(table_ref[at : at + 1, half : half + 128], 8)
-                for k in range(2):
-                    found[k][r] = jnp.where(chunk[k] == h, take(row, lane[k]), found[k][r])
-        for k in range(2):
-            here = pl.multiple_of(base + 8 * k, 8)
-            kept = [keep_ref[r, pl.ds(here, 8), :] for r in range(12)]
-            i0, i1, i2, i3, i4, i5, g0, g1, g2 = found[k]
-            p, q = kept[0:3], kept[3:6]
-            pv = [
-                i0 * p[0] + i1 * p[1] + i2 * p[2],
-                i1 * p[0] + i3 * p[1] + i4 * p[2],
-                i2 * p[0] + i4 * p[1] + i5 * p[2],
-            ]
-            qv = [
-                i0 * q[0] + i1 * q[1] + i2 * q[2],
-                i1 * q[0] + i3 * q[1] + i4 * q[2],
-                i2 * q[0] + i4 * q[1] + i5 * q[2],
-            ]
-            live = kept[11]
-            values = [
-                kept[8],
-                kept[9],
-                kept[10],
-                live - (pv[0] * p[0] + pv[1] * p[1] + pv[2] * p[2]),
-                -(pv[0] * q[0] + pv[1] * q[1] + pv[2] * q[2]),
-                live - (qv[0] * q[0] + qv[1] * q[1] + qv[2] * q[2]),
-                kept[6] - (p[0] * g0 + p[1] * g1 + p[2] * g2),
-                kept[7] - (q[0] * g0 + q[1] * g1 + q[2] * g2),
-            ]
-            for r, value in enumerate(values):
-                out_ref[pl.ds(here * 8 + r, 8, stride=8), :] = value
-        return carry
-
-    lax.fori_loop(0, 8, group, 0)
+    lax.fori_loop(0, 3, pick_pair, 0)
+    pick(7, 1)
+    finish_two(6, 0)
+    finish_two(7, 1)
 
 
 def exchange_out(vector_ref, slots_ref, edge_ref, weight_ref, out_ref, turn_ref, left_ref, hot_ref):
@@ -283,7 +335,7 @@
         index = spread(slots_ref[j : j + 1, :], 8)
         lane = index & 127
         turn_ref[8 * j : 8 * j + 8, :] = jnp.where(index >= 128, take(high, lane), take(low, lane))
-    out_ref[:, 0:128] = jnp.transpose(turn_ref[...])
+    out_ref[pl.ds(0, 128, stride=2), :] = jnp.transpose(turn_ref[...])
     iota = iota_bf16(128)
     for k in range(8):
         for h in range(2):
@@ -301,11 +353,11 @@
     summed = dot_lanes(hot_ref[...], left_ref[0])
     for n in range(1, PARTS):
         summed = summed + dot_lanes(hot_ref[...], left_ref[n])
-    out_ref[:, 128:256] = summed
+    out_ref[pl.ds(1, 128, stride=2), :] = summed
 
 
 def exchange_in(recv_ref, slots_ref, edge_ref, weight_ref, turn_ref, few_ref, cams_ref, near_ref):
-    turn_ref[...] = jnp.transpose(recv_ref[:, 0:128])
+    turn_ref[...] = jnp.transpose(recv_ref[pl.ds(0, 128, stride=2), :])
     for h in range(2):
         sums = jnp.zeros((8, 128), F32)
         for k in range(8):
@@ -317,7 +369,7 @@
             sums = sums + spread(weight_ref[k : k + 1, h * 128 : (h + 1) * 128], 8) * near
         near_ref[:, h * 128 : (h + 1) * 128] = sums
     scalar = jnp.sum(turn_ref[7:8, :], axis=1, keepdims=True)
-    turn_ref[...] = jnp.transpose(recv_ref[:, 128:256])
+    turn_ref[...] = jnp.transpose(recv_ref[pl.ds(1, 128, stride=2), :])
     iota = iota_bf16(256)
     for j in range(16):
         parts = parts_of(turn_ref[8 * j : 8 * j + 8, :])
@@ -356,9 +408,9 @@
 ):
     iota = iota_bf16(256)
     sum_ref[...] = jnp.zeros_like(sum_ref)
-    entry_ref[27 * 8 : 32 * 8, :] = jnp.zeros((40, 128), F32)
-
-    def build(t, side):
+    entry_ref[:, 27 * 8 : 32 * 8, :] = jnp.zeros((2, 40, 128), F32)
+
+    def build(t, side, half):
         base = pl.multiple_of(t * 8, 8)
         u, v, w, s00, s01, s11, f0, f1 = [
             recv_ref[pl.ds(base * 8 + r, 8, stride=8), :] for r in range(8)
@@ -370,28 +422,36 @@
         g = [s00 * top[k] + s01 * low[k] for k in range(6)]
         h = [s01 * top[k] + s11 * low[k] for k in range(6)]
         for r, (a, b) in enumerate(SYMMETRIC_PAIRS):
-            entry_ref[8 * r : 8 * r + 8, :] = top[a] * g[b] + low[a] * h[b]
+            entry_ref[half, 8 * r : 8 * r + 8, :] = top[a] * g[b] + low[a] * h[b]
         for a in range(6):
-            entry_ref[8 * (21 + a) : 8 * (22 + a), :] = top[a] * f0 + low[a] * f1
+            entry_ref[half, 8 * (21 + a) : 8 * (22 + a), :] = top[a] * f0 + low[a] * f1
         index = index_ref[pl.ds(base, 8), :].astype(F32)
         for i in range(8):
-            onehot_rows(hot_ref.at[side], index[i : i + 1, :], 256, i * 128, iota)
-            for n, part in enumerate(parts_of(entry_ref[pl.ds(i, 32, stride=8), :])):
-                left_ref[side, n * 32 : (n + 1) * 32, i * 128 : (i + 1) * 128] = part.astype(BF16)
+            onehot_rows(hot_ref.at[side], index[i : i + 1, :], 256, half * 1024 + i * 128, iota)
+            at = half * 1024 + i * 128
+            for n, part in enumerate(parts_of(entry_ref[half, pl.ds(i, 32, stride=8), :])):
+                left_ref[side, n * 32 : (n + 1) * 32, at : at + 128] = part.astype(BF16)
+
+    def build_two(g, side):
+        build(2 * g, side, 0)
+        build(2 * g + 1, side, 1)
 
     def product(side):
         sum_ref[...] += dot_lanes(left_ref[side], hot_ref[side])
 
-    build(0, 0)
-
-    def pair(t, carry):
-        build(2 * t + 1, 1)
+    build_two(0, 0)
+
+    def pair(p, carry):
+        build_two(2 * p + 1, 1)
         product(0)
-        build(jnp.minimum(2 * t + 2, 15), 0)
+        build_two(2 * p + 2, 0)
         product(1)
         return carry
 
-    lax.fori_loop(0, 8, pair, 0)
+    lax.fori_loop(0, 3, pair, 0)
+    build_two(7, 1)
+    product(0)
+    product(1)
     summed = sum_ref[0:32, :]
     for n in range(1, PARTS):
         summed = summed + sum_ref[32 * n : 32 * n + 32, :]
@@ -486,62 +546,91 @@
     residual_ref[...] = state_ref[0:6, :] - alpha_next * (state_ref[16:22, :] + beta * image)
 
 
+def kernels():
+    vmem = pltpu.VMEM
+    return {
+        "poses": call(
+            pose_kernel,
+            "poses",
+            array(1024, 128),
+            [
+                vmem((7, 256), F32),
+                vmem((128, 128), jnp.int32),
+                vmem((2, 128, 128), F32),
+            ]
+            + [pltpu.SemaphoreType.DMA] * 3,
+            in_specs=[pl.BlockSpec(memory_space=pltpu.HBM)] * 3,
+        ),
+        "positions": call(position_kernel, "positions", array(3, 128, 128)),
+        "eliminate": call(
+            eliminate_kernel,
+            "eliminate",
+            array(1024, 128),
+            [
+                vmem((16, 72, 128), F32),
+                vmem((12, 128, 128), F32),
+                vmem((2, 288, 2048), BF16),
+                vmem((16, 256, 1024), BF16),
+                vmem((288, 256), F32),
+                vmem((288, 128), F32),
+                vmem((128, 128), F32),
+                vmem((16, 256), F32),
+                vmem((256, 256), BF16),
+                vmem((2, 256, 2048), F32),
+                vmem((2, 64, 128), F32),
+            ],
+        ),
+        "cameras": call(
+            camera_kernel,
+            "cameras",
+            (array(256, 128), array(32, 256), array(8, 256)),
+            [
+                vmem((2, 256, 128), F32),
+                vmem((2, 32 * PARTS, 2048), BF16),
+                vmem((2, 256, 2048), BF16),
+                vmem((32 * PARTS, 256), F32),
+            ]
+            + OUT_SCRATCH,
+        ),
+        "first": call(
+            first_kernel,
+            "first_product",
+            (array(256, 128), array(8, 256), array(8, 256)),
+            OUT_SCRATCH + IN_SCRATCH,
+        ),
+        "second": call(
+            second_kernel,
+            "second_product",
+            (array(128, 128), array(24, 256)),
+            [OUT_SCRATCH[0]] + IN_SCRATCH,
+        ),
+        "last": call(last_kernel, "last", (array(6, 256), array(6, 256))),
+    }
+
+
 def swap(payload):
-    return lax.all_to_all(payload, AXES, split_axis=0, concat_axis=0, tiled=True)
+    blocks = payload.reshape(128, payload.shape[0] // 128, 128)
+    return lax.all_to_all(blocks, AXES, split_axis=0, concat_axis=0, tiled=True).reshape(
+        payload.shape
+    )
 
 
 def per_device(
     cam_pose, points, obs_uv, obs_cam, obs_pt, block_count, send_list, edge_slot, edge_weight
 ):
+    run = kernels()
     cam_index = obs_cam.reshape(128, 128)
     point_index = obs_pt.reshape(128, 128)
-    slots = jnp.transpose(send_list.reshape(128, 16))
-    poses = call(pose_kernel, "poses", array(1024, 128), [pltpu.VMEM((8, 256), F32)])(
-        cam_pose, cam_index, obs_uv.reshape(2, 128, 128)
-    )
-    arrived = swap(poses.reshape(128, 8, 128)).reshape(1024, 128)
-    position = call(position_kernel, "positions", array(3, 128, 128))(points, point_index)
-    reduced = call(
-        eliminate_kernel,
-        "eliminate",
-        array(1024, 128),
-        [
-            pltpu.VMEM((9, 128, 128), F32),
-            pltpu.VMEM((12, 128, 128), F32),
-            pltpu.VMEM((2, 144 * PARTS, 1024), BF16),
-            pltpu.VMEM((2, 256, 1024), BF16),
-            pltpu.VMEM((144 * PARTS, 256), F32),
-            pltpu.VMEM((144, 256), F32),
-        ],
-    )(arrived, position, point_index, block_count)
-    returned = swap(reduced.reshape(128, 8, 128)).reshape(1024, 128)
-    payload, system, vector = call(
-        camera_kernel,
-        "cameras",
-        (array(128, 256), array(32, 256), array(8, 256)),
-        [
-            pltpu.VMEM((256, 128), F32),
-            pltpu.VMEM((2, 32 * PARTS, 1024), BF16),
-            pltpu.VMEM((2, 256, 1024), BF16),
-            pltpu.VMEM((32 * PARTS, 256), F32),
-        ]
-        + OUT_SCRATCH,
-    )(returned, cam_index, slots, edge_slot, edge_weight)
-    payload, image, following = call(
-        first_kernel,
-        "first_product",
-        (array(128, 256), array(8, 256), array(8, 256)),
-        OUT_SCRATCH + IN_SCRATCH,
-    )(swap(payload), system, vector, slots, edge_slot, edge_weight)
-    payload, state = call(
-        second_kernel,
-        "second_product",
-        (array(128, 128), array(24, 256)),
-        [OUT_SCRATCH[0]] + IN_SCRATCH,
-    )(swap(payload), system, vector, image, following, slots, edge_slot, edge_weight)
-    return call(last_kernel, "last", (array(6, 256), array(6, 256)))(
-        swap(payload.reshape(128, 1, 128)).reshape(128, 128), vector, image, state
-    )
+    graph = (jnp.transpose(send_list.reshape(128, 16)), edge_slot, edge_weight)
+    poses = run["poses"](cam_pose, cam_index, obs_uv.reshape(2, 128, 128))
+    arrived = swap(poses)
+    position = run["positions"](points, point_index)
+    reduced = run["eliminate"](arrived, position, point_index, block_count)
+    returned = swap(reduced)
+    payload, system, vector = run["cameras"](returned, cam_index, *graph)
+    payload, image, following = run["first"](swap(payload), system, vector, *graph)
+    payload, state = run["second"](swap(payload), system, vector, image, following, *graph)
+    return run["last"](swap(payload), vector, image, state)
 
 
 def solution(mesh):

time: 115 us -> 109 us (0.948)
  Pallas kernels: 30.4 us -> 21.8 us
  waiting for transfers between devices: 9.13 us -> 11.7 us
    pallas_call x7, Pallas kernels: 30.4 us -> 21.8 us  [the longest x1 9.95 us: per_device(): reduced = run['eliminate'](arrived, position, point_index, block_count)]
    all_to_all x1, waiting for transfers between devices: 9.13 us -> 11.7 us  [swap(): lax.all_to_all(blocks, AXES, split_axis=0, concat_axis=0, tiled=True)]
    unnamed x22 -> x20, local copies, waits for them, and re-layouts: 2.49 us -> 2.48 us
  transfers between devices with their start and end apart: 1 -> 1, of which waited for: 1 -> 1; matrix products, arithmetic and copies ran while one was open for 0% -> 0% of each run, Pallas kernels for 4% -> 2%
where the time goes in v2:
time: 109 us
  blocking collectives  60.4 us (55%)
  Pallas kernels  21.8 us (20%)
  waiting for transfers between devices  11.7 us (11%)
  starting transfers between devices  11.5 us (11%)
  local copies, waits for them, and re-layouts  2.48 us (2%)
    all_to_all x4, blocking collectives, swap(): lax.all_to_all(blocks, AXES, split_axis=0, concat_axis=0, tiled=True)  60.4 us
    all_to_all x1, waiting for transfers between devices, swap(): lax.all_to_all(blocks, AXES, split_axis=0, concat_axis=0, tiled=True)  11.7 us
    all_to_all x1, starting transfers between devices, swap(): lax.all_to_all(blocks, AXES, split_axis=0, concat_axis=0, tiled=True)  11.5 us
    pallas_call x1, Pallas kernels, per_device(): reduced = run['eliminate'](arrived, position, point_index, block_count)  9.95 us
    pallas_call x1, Pallas kernels, per_device(): payload, system, vector = run['cameras'](returned, cam_index, *graph)  4.98 us
    unnamed x20, local copies, waits for them, and re-layouts  2.48 us
  transfers between devices with their start and end apart: 1, of which 1 were waited for; matrix products, arithmetic and copies ran while one was open for 0% of the time, Pallas kernels for 2%

profile of v2, /device:TPU:1, one launch (start us, length us, event | category | flops | bytes accessed | tf_op | source)
XLA Modules:
  0.0 108.7 jit_solution(1758666113113101974)
XLA Ops:
  0.6 0.0 copy-start.1
  0.6 0.8 copy-done.1
  1.5 0.0 copy-start.3
  1.5 0.9 copy-done.3
  2.4 0.7 copy-done.8
  3.1 1.6 %poses.1 = f32[1024,128]{1,0:T(8,128)} custom-call(f32[7,256]{1,0:T(8,128)S(1)} %copy-done.8, s32[128,128]{1,0:T(8,128)S(1)} %bitcast.25, f32[2,128,128]{2,1,0:T(8,128)S(1)} %bitcast.30), custom_call_target="tpu_custom_call" | custom-call | flops 1000000 | bytes 1000000 | tf_op jit(solution)/shard_map/poses/pallas_call | solution.py:625
  4.7 0.0 copy-start
  4.7 0.0 copy-start.7
  4.7 11.5 %all-to-all-start = ((f32[128,8,128]{2,1,0:T(8,128)}), f32[128,8,128]{2,1,0:T(8,128)S(1)}, u32[]{:S(2)}, u32[]{:S(2)}) async-start(f32[128,8,128]{2,1,0:T(8,128)} %bitcast.2), calls=%async_computation | async-start | bytes 1048576 | tf_op jit(solution)/shard_map/all_to_all | solution.py:613
  16.2 0.0 copy-done
  16.2 0.0 copy-done.7
  16.2 1.9 %positions.1.position_ref = f32[3,128,128]{2,1,0:T(8,128)S(1)} custom-call(f32[3,4096]{1,0:T(4,128)S(1)} %copy-done.7, s32[128,128]{1,0:T(8,128)S(1)} %bitcast.23), custom_call_target="tpu_custom_call" | custom-call | flops 1000000 | bytes 1000000 | tf_op jit(solution)/shard_map/positions/pallas_call | solution.py:627
  18.2 0.0 copy-start.9
  18.2 11.7 %all-to-all-done = f32[128,8,128]{2,1,0:T(8,128)S(1)} async-done(((f32[128,8,128]{2,1,0:T(8,128)}), f32[128,8,128]{2,1,0:T(8,128)S(1)}, u32[]{:S(2)}, u32[]{:S(2)}) %all-to-all-start) | async-done | bytes 524320 | tf_op jit(solution)/shard_map/all_to_all | solution.py:613
  29.9 0.0 copy-done.9
  29.9 9.9 %eliminate.1 = f32[1024,128]{1,0:T(8,128)S(1)} custom-call(f32[1024,128]{1,0:T(8,128)S(1)} %bitcast.18, f32[3,128,128]{2,1,0:T(8,128)S(1)} %positions.1.position_ref, s32[128,128]{1,0:T(8,128)S(1)} %bitcast.24, s32[1,128]{1,0:T(1,128)S(1)} %copy-done.9), custom_call_target="tpu_custom_call" | custom-call | flops 1000000 | bytes 1000000 | tf_op jit(solution)/shard_map/eliminate/pallas_call | solution.py:628
  39.9 0.0 copy-start.2
  39.9 0.0 copy-start.4
  39.9 0.0 copy-start.5
  39.9 0.0 copy-start.6
  39.9 18.0 %all_to_all.25 = f32[128,8,128]{2,1,0:T(8,128)S(1)} all-to-all(f32[128,8,128]{2,1,0:T(8,128)S(1)} %bitcast.19), channel_id=1, replica_groups=mesh['gx'=4,'gy'=32] {'gx','gy'}, dimensions={0} | all-to-all | bytes 1048576 | tf_op jit(solution)/shard_map/all_to_all | solution.py:613
  58.0 0.0 copy-done.2
  58.0 0.0 copy-done.4
  58.0 0.0 copy-done.5
  58.0 0.0 copy-done.6
  58.0 5.0 %cameras.1 = (f32[256,128]{1,0:T(8,128)S(1)}, f32[32,256]{1,0:T(8,128)S(1)}, f32[8,256]{1,0:T(8,128)S(1)}) custom-call(f32[1024,128]{1,0:T(8,128)S(1)} %bitcast.20, s32[128,128]{1,0:T(8,128)S(1)} %bitcast.26, s32[16,128]{1,0:T(8,128)S(1)} %bitcast.31, s32[8,256]{1,0:T(8,128)S(1)} %copy-done.5, f32[8,256]{1,0:T(8,128)S(1)} %copy-done.6), custom_call_target="tpu_custom_call" | custom-call | flops 1000000 | bytes 1000000 | tf_op jit(solution)/shard_map/cameras/pallas_call | solution.py:630
  63.0 14.4 %all_to_all.26 = f32[128,2,128]{2,1,0:T(2,128)S(1)} all-to-all(f32[128,2,128]{2,1,0:T(2,128)S(1)} %bitcast.28), channel_id=1, replica_groups=mesh['gx'=4,'gy'=32] {'gx','gy'}, dimensions={0} | all-to-all | bytes 262144 | tf_op jit(solution)/shard_map/all_to_all | solution.py:613
  77.4 1.7 %first_product.1 = (f32[256,128]{1,0:T(8,128)S(1)}, f32[8,256]{1,0:T(8,128)S(1)}, f32[8,256]{1,0:T(8,128)S(1)}) custom-call(f32[256,128]{1,0:T(8,128)S(1)} %bitcast.22, f32[32,256]{1,0:T(8,128)S(1)} %get-tuple-element.11.system_ref, f32[8,256]{1,0:T(8,128)S(1)} %get-tuple-element.12.vector_ref, s32[16,128]{1,0:T(8,128)S(1)} %bitcast.32, ...), custom_call_target="tpu_custom_call" | custom-call | flops 1000000 | bytes 1000000 | tf_op jit(solution)/shard_map/first_product/pallas_call | solution.py:631
  79.1 14.3 %all_to_all.27 = f32[128,2,128]{2,1,0:T(2,128)S(1)} all-to-all(f32[128,2,128]{2,1,0:T(2,128)S(1)} %bitcast.29), channel_id=1, replica_groups=mesh['gx'=4,'gy'=32] {'gx','gy'}, dimensions={0} | all-to-all | bytes 262144 | tf_op jit(solution)/shard_map/all_to_all | solution.py:613
  93.3 0.8 second_product.1
  94.1 13.7 %all_to_all.28 = f32[128,1,128]{2,1,0:T(1,128)S(1)} all-to-all(f32[128,1,128]{2,1,0:T(1,128)S(1)} %bitcast.34), channel_id=1, replica_groups=mesh['gx'=4,'gy'=32] {'gx','gy'}, dimensions={0} | all-to-all | bytes 131072 | tf_op jit(solution)/shard_map/all_to_all | solution.py:613
  107.8 0.9 last.1
  (1 shorter events, 0.0 us)
Async XLA Ops:
  0.6 0.8 copy-start.1
  1.5 0.9 copy-start.3
  2.4 0.7 copy-start.8
  4.7 11.5 %copy-start = (s32[1,128,128]{2,1,0:T(8,128)S(1)}, s32[1,128,128]{2,1,0:T(8,128)}, u32[]{:S(2)}) copy-start(s32[1,128,128]{2,1,0:T(8,128)} %param.13) | copy-start | bytes 196612
  4.7 11.5 %copy-start.7 = (f32[3,4096]{1,0:T(4,128)S(1)}, f32[3,4096]{1,0:T(4,128)}, u32[]{:S(2)}) copy-start(f32[3,4096]{1,0:T(4,128)} %points_ref.1) | copy-start | bytes 147460
  4.7 25.2 %all-to-all-start = ((f32[128,8,128]{2,1,0:T(8,128)}), f32[128,8,128]{2,1,0:T(8,128)S(1)}, u32[]{:S(2)}, u32[]{:S(2)}) async-start(f32[128,8,128]{2,1,0:T(8,128)} %bitcast.2), calls=%async_computation | async-start | bytes 1048576 | tf_op jit(solution)/shard_map/all_to_all | solution.py:613
  18.2 11.8 %copy-start.9 = (s32[1,128]{1,0:T(1,128)S(1)}, s32[1,128]{1,0:T(1,128)}, u32[]{:S(2)}) copy-start(s32[1,128]{1,0:T(1,128)} %count_ref.1) | copy-start | bytes 1540
  39.9 18.1 %copy-start.2 = (s32[1,128,128]{2,1,0:T(8,128)S(1)}, s32[1,128,128]{2,1,0:T(8,128)}, u32[]{:S(2)}) copy-start(s32[1,128,128]{2,1,0:T(8,128)} %param.12) | copy-start | bytes 196612
  39.9 18.1 %copy-start.4 = (s32[1,128,16]{1,2,0:T(8,128)S(1)}, s32[1,128,16]{1,2,0:T(8,128)}, u32[]{:S(2)}) copy-start(s32[1,128,16]{1,2,0:T(8,128)} %param.15) | copy-start | bytes 24580
  39.9 18.1 %copy-start.5 = (s32[8,256]{1,0:T(8,128)S(1)}, s32[8,256]{1,0:T(8,128)}, u32[]{:S(2)}) copy-start(s32[8,256]{1,0:T(8,128)} %edge_ref.5) | copy-start | bytes 24580
  39.9 18.1 %copy-start.6 = (f32[8,256]{1,0:T(8,128)S(1)}, f32[8,256]{1,0:T(8,128)}, u32[]{:S(2)}) copy-start(f32[8,256]{1,0:T(8,128)} %weight_ref.5) | copy-start | bytes 24580

commit v3 on v2

--- a/solution.py
+++ b/solution.py
@@ -22,7 +22,7 @@
 
 
 def call(
-    kernel, name, out_shape, scratch=(), flops=1_000_000, bytes_accessed=1_000_000, **specs
+    kernel, name, out_shape, scratch=(), flops=1_000_000, bytes_accessed=1_000_000, vmem=48, **specs
 ):
     return pl.pallas_call(
         kernel,
@@ -30,7 +30,9 @@
         **specs,
         scratch_shapes=list(scratch),
         name=name,
-        compiler_params=pltpu.CompilerParams(vmem_limit_bytes=48 * 1024 * 1024),
+        compiler_params=pltpu.CompilerParams(
+            vmem_limit_bytes=vmem * 1024 * 1024 if vmem else None
+        ),
         cost_estimate=pl.CostEstimate(
             flops=flops, bytes_accessed=bytes_accessed, transcendentals=0
         ),
@@ -177,7 +179,7 @@
             keep_ref[r, pl.ds(base, 8), :] = value
         return carry
 
-    lax.fori_loop(0, 16, prepare, 0)
+    lax.fori_loop(0, 16, prepare, 0, unroll=4)
 
     iota_chunk, iota_lane = iota_bf16(16), iota_bf16(256)
     zero = jnp.zeros((), BF16)
@@ -406,7 +408,7 @@
     recv_ref, index_ref, slots_ref, edge_ref, weight_ref, out_ref, system_ref, vector_ref,
     entry_ref, left_ref, hot_ref, sum_ref, turn_ref, edge_left_ref, edge_hot_ref,
 ):
-    iota = iota_bf16(256)
+    iota = iota_bf16(128)
     sum_ref[...] = jnp.zeros_like(sum_ref)
     entry_ref[:, 27 * 8 : 32 * 8, :] = jnp.zeros((2, 40, 128), F32)
 
@@ -425,12 +427,19 @@
             entry_ref[half, 8 * r : 8 * r + 8, :] = top[a] * g[b] + low[a] * h[b]
         for a in range(6):
             entry_ref[half, 8 * (21 + a) : 8 * (22 + a), :] = top[a] * f0 + low[a] * f1
-        index = index_ref[pl.ds(base, 8), :].astype(F32)
+        index = index_ref[pl.ds(base, 8), :]
+        lane = (index & 127).astype(F32)
         for i in range(8):
-            onehot_rows(hot_ref.at[side], index[i : i + 1, :], 256, half * 1024 + i * 128, iota)
             at = half * 1024 + i * 128
+            onehot_rows(hot_ref.at[side], lane[i : i + 1, :], 128, at, iota)
+            above = spread(index[i : i + 1, :], 32) >= 128
             for n, part in enumerate(parts_of(entry_ref[half, pl.ds(i, 32, stride=8), :])):
-                left_ref[side, n * 32 : (n + 1) * 32, at : at + 128] = part.astype(BF16)
+                left_ref[side, n * 32 : (n + 1) * 32, at : at + 128] = jnp.where(
+                    above, 0.0, part
+                ).astype(BF16)
+                left_ref[side, 64 + n * 32 : 96 + n * 32, at : at + 128] = jnp.where(
+                    above, part, 0.0
+                ).astype(BF16)
 
     def build_two(g, side):
         build(2 * g, side, 0)
@@ -452,10 +461,11 @@
     build_two(7, 1)
     product(0)
     product(1)
-    summed = sum_ref[0:32, :]
-    for n in range(1, PARTS):
-        summed = summed + sum_ref[32 * n : 32 * n + 32, :]
-    system_ref[0:32, :] = summed
+    for h in range(2):
+        at = 32 * PARTS * h
+        system_ref[:, h * 128 : h * 128 + 128] = sum(
+            sum_ref[at + 32 * n : at + 32 * n + 32, :] for n in range(PARTS)
+        )
     partial = jnp.zeros((1, 256), F32)
     for a in range(6):
         at = LOOKUP[a, a]
@@ -559,7 +569,8 @@
                 vmem((2, 128, 128), F32),
             ]
             + [pltpu.SemaphoreType.DMA] * 3,
-            in_specs=[pl.BlockSpec(memory_space=pltpu.HBM)] * 3,
+            in_specs=[pl.BlockSpec(memory_space=pl.ANY)] * 3,
+            vmem=None,
         ),
         "positions": call(position_kernel, "positions", array(3, 128, 128)),
         "eliminate": call(
@@ -586,9 +597,9 @@
             (array(256, 128), array(32, 256), array(8, 256)),
             [
                 vmem((2, 256, 128), F32),
-                vmem((2, 32 * PARTS, 2048), BF16),
-                vmem((2, 256, 2048), BF16),
-                vmem((32 * PARTS, 256), F32),
+                vmem((2, 64 * PARTS, 2048), BF16),
+                vmem((2, 128, 2048), BF16),
+                vmem((64 * PARTS, 128), F32),
             ]
             + OUT_SCRATCH,
         ),

time: 109 us -> 106 us (0.972)
  local copies, waits for them, and re-layouts: 2.48 us -> 0.04 us
    unnamed x20 -> x14, local copies, waits for them, and re-layouts: 2.48 us -> 0.04 us
where the time goes in v3:
time: 106 us
  blocking collectives  60.4 us (57%)
  Pallas kernels  21.7 us (20%)
  waiting for transfers between devices  11.7 us (11%)
  starting transfers between devices  11.5 us (11%)
    all_to_all x4, blocking collectives, swap(): lax.all_to_all(blocks, AXES, split_axis=0, concat_axis=0, tiled=True)  60.4 us
    all_to_all x1, waiting for transfers between devices, swap(): lax.all_to_all(blocks, AXES, split_axis=0, concat_axis=0, tiled=True)  11.7 us
    all_to_all x1, starting transfers between devices, swap(): lax.all_to_all(blocks, AXES, split_axis=0, concat_axis=0, tiled=True)  11.5 us
    pallas_call x1, Pallas kernels, per_device(): reduced = run['eliminate'](arrived, position, point_index, block_count)  9.76 us
    pallas_call x1, Pallas kernels, per_device(): payload, system, vector = run['cameras'](returned, cam_index, *graph)  4.31 us
    pallas_call x1, Pallas kernels, per_device(): poses = run['poses'](cam_pose, cam_index, obs_uv.reshape(2, 128, 128))  2.31 us
  transfers between devices with their start and end apart: 1, of which 1 were waited for; matrix products, arithmetic and copies ran while one was open for 0% of the time, Pallas kernels for 2%

profile of v3, /device:TPU:1, one launch (start us, length us, event | category | flops | bytes accessed | tf_op | source)
XLA Modules:
  0.0 106.1 jit_solution(11008779924162012565)
XLA Ops:
  0.6 2.3 %poses.1 = f32[1024,128]{1,0:T(8,128)} custom-call(f32[7,256]{1,0:T(8,128)} %pose_hbm.1, s32[128,128]{1,0:T(8,128)} %bitcast.25, f32[2,128,128]{2,1,0:T(8,128)} %bitcast.35), custom_call_target="tpu_custom_call" | custom-call | flops 1000000 | bytes 1000000 | tf_op jit(solution)/shard_map/poses/pallas_call | solution.py:636
  2.9 0.0 copy-start
  3.0 0.0 copy-start.5
  3.0 11.5 %all-to-all-start = ((f32[128,8,128]{2,1,0:T(8,128)}), f32[128,8,128]{2,1,0:T(8,128)S(1)}, u32[]{:S(2)}, u32[]{:S(2)}) async-start(f32[128,8,128]{2,1,0:T(8,128)} %bitcast.34), calls=%async_computation | async-start | bytes 1048576 | tf_op jit(solution)/shard_map/all_to_all | solution.py:624
  14.5 0.0 copy-done
  14.5 0.0 copy-done.5
  14.5 1.9 %positions.1.position_ref = f32[3,128,128]{2,1,0:T(8,128)S(1)} custom-call(f32[3,4096]{1,0:T(4,128)S(1)} %copy-done.5, s32[128,128]{1,0:T(8,128)S(1)} %bitcast.23), custom_call_target="tpu_custom_call" | custom-call | flops 1000000 | bytes 1000000 | tf_op jit(solution)/shard_map/positions/pallas_call | solution.py:638
  16.5 0.0 copy-start.6
  16.5 11.7 %all-to-all-done = f32[128,8,128]{2,1,0:T(8,128)S(1)} async-done(((f32[128,8,128]{2,1,0:T(8,128)}), f32[128,8,128]{2,1,0:T(8,128)S(1)}, u32[]{:S(2)}, u32[]{:S(2)}) %all-to-all-start) | async-done | bytes 524320 | tf_op jit(solution)/shard_map/all_to_all | solution.py:624
  28.2 0.0 copy-done.6
  28.2 9.8 %eliminate.1 = f32[1024,128]{1,0:T(8,128)S(1)} custom-call(f32[1024,128]{1,0:T(8,128)S(1)} %bitcast.18, f32[3,128,128]{2,1,0:T(8,128)S(1)} %positions.1.position_ref, s32[128,128]{1,0:T(8,128)S(1)} %bitcast.24, s32[1,128]{1,0:T(1,128)S(1)} %copy-done.6), custom_call_target="tpu_custom_call" | custom-call | flops 1000000 | bytes 1000000 | tf_op jit(solution)/shard_map/eliminate/pallas_call | solution.py:639
  38.0 0.0 copy-start.1
  38.0 0.0 copy-start.2
  38.0 0.0 copy-start.3
  38.0 0.0 copy-start.4
  38.0 18.0 %all_to_all.25 = f32[128,8,128]{2,1,0:T(8,128)S(1)} all-to-all(f32[128,8,128]{2,1,0:T(8,128)S(1)} %bitcast.19), channel_id=1, replica_groups=mesh['gx'=4,'gy'=32] {'gx','gy'}, dimensions={0} | all-to-all | bytes 1048576 | tf_op jit(solution)/shard_map/all_to_all | solution.py:624
  56.1 0.0 copy-done.1
  56.1 0.0 copy-done.2
  56.1 0.0 copy-done.3
  56.1 0.0 copy-done.4
  56.1 4.3 %cameras.1 = (f32[256,128]{1,0:T(8,128)S(1)}, f32[32,256]{1,0:T(8,128)S(1)}, f32[8,256]{1,0:T(8,128)S(1)}) custom-call(f32[1024,128]{1,0:T(8,128)S(1)} %bitcast.20, s32[128,128]{1,0:T(8,128)S(1)} %bitcast.26, s32[16,128]{1,0:T(8,128)S(1)} %bitcast.30, s32[8,256]{1,0:T(8,128)S(1)} %copy-done.3, f32[8,256]{1,0:T(8,128)S(1)} %copy-done.4), custom_call_target="tpu_custom_call" | custom-call | flops 1000000 | bytes 1000000 | tf_op jit(solution)/shard_map/cameras/pallas_call | solution.py:641
  60.4 14.4 %all_to_all.26 = f32[128,2,128]{2,1,0:T(2,128)S(1)} all-to-all(f32[128,2,128]{2,1,0:T(2,128)S(1)} %bitcast.28), channel_id=1, replica_groups=mesh['gx'=4,'gy'=32] {'gx','gy'}, dimensions={0} | all-to-all | bytes 262144 | tf_op jit(solution)/shard_map/all_to_all | solution.py:624
  74.8 1.7 %first_product.1 = (f32[256,128]{1,0:T(8,128)S(1)}, f32[8,256]{1,0:T(8,128)S(1)}, f32[8,256]{1,0:T(8,128)S(1)}) custom-call(f32[256,128]{1,0:T(8,128)S(1)} %bitcast.22, f32[32,256]{1,0:T(8,128)S(1)} %get-tuple-element.11.system_ref, f32[8,256]{1,0:T(8,128)S(1)} %get-tuple-element.12.vector_ref, s32[16,128]{1,0:T(8,128)S(1)} %bitcast.31, ...), custom_call_target="tpu_custom_call" | custom-call | flops 1000000 | bytes 1000000 | tf_op jit(solution)/shard_map/first_product/pallas_call | solution.py:642
  76.5 14.3 %all_to_all.27 = f32[128,2,128]{2,1,0:T(2,128)S(1)} all-to-all(f32[128,2,128]{2,1,0:T(2,128)S(1)} %bitcast.29), channel_id=1, replica_groups=mesh['gx'=4,'gy'=32] {'gx','gy'}, dimensions={0} | all-to-all | bytes 262144 | tf_op jit(solution)/shard_map/all_to_all | solution.py:624
  90.8 0.8 second_product.1
  91.5 13.7 %all_to_all.28 = f32[128,1,128]{2,1,0:T(1,128)S(1)} all-to-all(f32[128,1,128]{2,1,0:T(1,128)S(1)} %bitcast.33), channel_id=1, replica_groups=mesh['gx'=4,'gy'=32] {'gx','gy'}, dimensions={0} | all-to-all | bytes 131072 | tf_op jit(solution)/shard_map/all_to_all | solution.py:624
  105.3 0.9 last.1
Async XLA Ops:
  2.9 11.5 %copy-start = (s32[1,128,128]{2,1,0:T(8,128)S(1)}, s32[1,128,128]{2,1,0:T(8,128)}, u32[]{:S(2)}) copy-start(s32[1,128,128]{2,1,0:T(8,128)} %param.13) | copy-start | bytes 196612
  3.0 11.5 %copy-start.5 = (f32[3,4096]{1,0:T(4,128)S(1)}, f32[3,4096]{1,0:T(4,128)}, u32[]{:S(2)}) copy-start(f32[3,4096]{1,0:T(4,128)} %points_ref.1) | copy-start | bytes 147460
  3.0 25.2 %all-to-all-start = ((f32[128,8,128]{2,1,0:T(8,128)}), f32[128,8,128]{2,1,0:T(8,128)S(1)}, u32[]{:S(2)}, u32[]{:S(2)}) async-start(f32[128,8,128]{2,1,0:T(8,128)} %bitcast.34), calls=%async_computation | async-start | bytes 1048576 | tf_op jit(solution)/shard_map/all_to_all | solution.py:624
  16.5 11.8 %copy-start.6 = (s32[1,128]{1,0:T(1,128)S(1)}, s32[1,128]{1,0:T(1,128)}, u32[]{:S(2)}) copy-start(s32[1,128]{1,0:T(1,128)} %count_ref.1) | copy-start | bytes 1540
  38.0 18.1 %copy-start.1 = (s32[1,128,128]{2,1,0:T(8,128)S(1)}, s32[1,128,128]{2,1,0:T(8,128)}, u32[]{:S(2)}) copy-start(s32[1,128,128]{2,1,0:T(8,128)} %param.12) | copy-start | bytes 196612
  38.0 18.1 %copy-start.2 = (s32[1,128,16]{1,2,0:T(8,128)S(1)}, s32[1,128,16]{1,2,0:T(8,128)}, u32[]{:S(2)}) copy-start(s32[1,128,16]{1,2,0:T(8,128)} %param.15) | copy-start | bytes 24580
  38.0 18.1 %copy-start.3 = (s32[8,256]{1,0:T(8,128)S(1)}, s32[8,256]{1,0:T(8,128)}, u32[]{:S(2)}) copy-start(s32[8,256]{1,0:T(8,128)} %edge_ref.5) | copy-start | bytes 24580
  38.0 18.1 %copy-start.4 = (f32[8,256]{1,0:T(8,128)S(1)}, f32[8,256]{1,0:T(8,128)}, u32[]{:S(2)}) copy-start(f32[8,256]{1,0:T(8,128)} %weight_ref.5) | copy-start | bytes 24580

commit v4 on v3

--- a/solution.py
+++ b/solution.py
@@ -41,6 +41,10 @@
 
 def array(*shape):
     return jax.ShapeDtypeStruct(shape, F32)
+
+
+def eight(t):
+    return t * 8 if isinstance(t, int) else pl.multiple_of(t * 8, 8)
 
 
 def take(table, index):
@@ -132,7 +136,7 @@
 
 def eliminate_kernel(
     recv_ref, position_ref, index_ref, count_ref, out_ref, term_ref, keep_ref, left_ref, hot_ref,
-    sum_ref, half_ref, table_ref, ninth_ref, parts_ref, picked_ref, found_ref,
+    sum_ref, half_ref, table_ref, rest_ref, parts_ref, picked_ref, found_ref,
 ):
     live_count = jnp.transpose(spread(count_ref[0:1, :], 128))
     keep_ref[11, :, :] = jnp.where(
@@ -251,10 +255,13 @@
             inv[1] * grad[0] + inv[3] * grad[1] + inv[4] * grad[2],
             inv[2] * grad[0] + inv[4] * grad[1] + inv[5] * grad[2],
         ]
-        for r, value in enumerate(inv + solved[0:2]):
-            table_ref[pl.ds(r, 16, stride=8), :] = value
-        ninth_ref[:, lanes] = solved[2]
-        for h in range(16):
+        for r, value in enumerate(inv[0:4]):
+            table_ref[pl.ds(r, 16, stride=4), :] = value
+        for r, value in enumerate(inv[4:6]):
+            table_ref[pl.ds(64 + r, 16, stride=2), :] = value
+        for r, value in enumerate(solved):
+            rest_ref[16 * r : 16 * r + 16, lanes] = value
+        for h in range(12):
             parts_ref[h * 16 : (h + 1) * 16, lanes] = jnp.concatenate(
                 parts_of(table_ref[8 * h : 8 * h + 8, :]), 0
             ).astype(BF16)
@@ -263,29 +270,45 @@
         picked_ref[side] = jnp.dot(parts_ref[...], hot_two(g), preferred_element_type=F32)
 
     def finish(t, side, half):
-        base = pl.multiple_of(t * 8, 8)
+        base = eight(t)
         index = index_ref[pl.ds(base, 8), :]
         chunk = index >> 8
+
+        def rows_of(first_row, count, where, at):
+            parts = [jnp.zeros((8, 128), F32) for _ in range(PARTS)]
+            for h in range(count):
+                for n in range(PARTS):
+                    row = first_row + 16 * h + 8 * n
+                    parts[n] = jnp.where(
+                        where == h, picked_ref[side, row : row + 8, at : at + 128], parts[n]
+                    )
+            return parts[0] + parts[1]
+
         for i in range(8):
             at = half * 1024 + i * 128
             where = spread(chunk[i : i + 1, :], 8)
-            first, second = jnp.zeros((8, 128), F32), jnp.zeros((8, 128), F32)
-            for h in range(16):
-                first = jnp.where(
-                    where == h, picked_ref[side, 16 * h : 16 * h + 8, at : at + 128], first
-                )
-                second = jnp.where(
-                    where == h, picked_ref[side, 16 * h + 8 : 16 * h + 16, at : at + 128], second
-                )
-            found_ref[half, 8 * i : 8 * i + 8, :] = first + second
+            four = rows_of(0, 8, where >> 1, at)
+            odd = spread(chunk[i : i + 1, :], 4) & 1
+            found_ref[half, 4 * i : 4 * i + 4, :] = jnp.where(
+                odd == 1, four[4:8, :], four[0:4, :]
+            )
+            two = rows_of(128, 4, where >> 2, at)
+            step = spread(chunk[i : i + 1, :], 2) & 3
+            found_ref[half, 32 + 2 * i : 34 + 2 * i, :] = jnp.where(
+                step >= 2,
+                jnp.where(step == 3, two[6:8, :], two[4:6, :]),
+                jnp.where(step == 1, two[2:4, :], two[0:2, :]),
+            )
         lane, chunk = index & 127, index >> 7
-        g2 = jnp.zeros((8, 128), F32)
+        rest = [jnp.zeros((8, 128), F32) for _ in range(3)]
         for h in range(32):
-            row = ninth_ref[h // 2 : h // 2 + 1, (h % 2) * 128 : (h % 2) * 128 + 128]
-            g2 = jnp.where(chunk == h, take(spread(row, 8), lane), g2)
-        i0, i1, i2, i3, i4, i5, g0, g1 = [
-            found_ref[half, pl.ds(r, 8, stride=8), :] for r in range(8)
-        ]
+            for r in range(3):
+                at = 16 * r + h // 2
+                row = rest_ref[at : at + 1, (h % 2) * 128 : (h % 2) * 128 + 128]
+                rest[r] = jnp.where(chunk == h, take(spread(row, 8), lane), rest[r])
+        g0, g1, g2 = rest
+        i0, i1, i2, i3 = [found_ref[half, pl.ds(r, 8, stride=4), :] for r in range(4)]
+        i4, i5 = [found_ref[half, pl.ds(32 + r, 8, stride=2), :] for r in range(2)]
         kept = [keep_ref[r, pl.ds(base, 8), :] for r in range(12)]
         p, q = kept[0:3], kept[3:6]
         pv = [
@@ -325,7 +348,8 @@
         finish_two(2 * p + 1, 1)
         return carry
 
-    lax.fori_loop(0, 3, pick_pair, 0)
+    for p in range(3):
+        pick_pair(p, 0)
     pick(7, 1)
     finish_two(6, 0)
     finish_two(7, 1)
@@ -584,11 +608,11 @@
                 vmem((16, 256, 1024), BF16),
                 vmem((288, 256), F32),
                 vmem((288, 128), F32),
-                vmem((128, 128), F32),
-                vmem((16, 256), F32),
-                vmem((256, 256), BF16),
-                vmem((2, 256, 2048), F32),
-                vmem((2, 64, 128), F32),
+                vmem((96, 128), F32),
+                vmem((48, 256), F32),
+                vmem((192, 256), BF16),
+                vmem((2, 192, 2048), F32),
+                vmem((2, 48, 128), F32),
             ],
         ),
         "cameras": call(

time: 106 us -> 106 us (level)
  no operation moved by 1% of the time
where the time goes in v4:
time: 106 us
  blocking collectives  60.4 us (57%)
  Pallas kernels  21.1 us (20%)
  waiting for transfers between devices  11.7 us (11%)
  starting transfers between devices  11.5 us (11%)
    all_to_all x4, blocking collectives, swap(): lax.all_to_all(blocks, AXES, split_axis=0, concat_axis=0, tiled=True)  60.4 us
    all_to_all x1, waiting for transfers between devices, swap(): lax.all_to_all(blocks, AXES, split_axis=0, concat_axis=0, tiled=True)  11.7 us
    all_to_all x1, starting transfers between devices, swap(): lax.all_to_all(blocks, AXES, split_axis=0, concat_axis=0, tiled=True)  11.5 us
    pallas_call x1, Pallas kernels, per_device(): reduced = run['eliminate'](arrived, position, point_index, block_count)  9.16 us
    pallas_call x1, Pallas kernels, per_device(): payload, system, vector = run['cameras'](returned, cam_index, *graph)  4.31 us
    pallas_call x1, Pallas kernels, per_device(): poses = run['poses'](cam_pose, cam_index, obs_uv.reshape(2, 128, 128))  2.31 us
  transfers between devices with their start and end apart: 1, of which 1 were waited for; matrix products, arithmetic and copies ran while one was open for 0% of the time, Pallas kernels for 2%

profile of v4, /device:TPU:1, one launch (start us, length us, event | category | flops | bytes accessed | tf_op | source)
XLA Modules:
  0.0 105.5 jit_solution(6290956843632482119)
XLA Ops:
  0.6 2.3 %poses.1 = f32[1024,128]{1,0:T(8,128)} custom-call(f32[7,256]{1,0:T(8,128)} %pose_hbm.1, s32[128,128]{1,0:T(8,128)} %bitcast.25, f32[2,128,128]{2,1,0:T(8,128)} %bitcast.35), custom_call_target="tpu_custom_call" | custom-call | flops 1000000 | bytes 1000000 | tf_op jit(solution)/shard_map/poses/pallas_call | solution.py:660
  2.9 0.0 copy-start
  3.0 0.0 copy-start.5
  3.0 11.5 %all-to-all-start = ((f32[128,8,128]{2,1,0:T(8,128)}), f32[128,8,128]{2,1,0:T(8,128)S(1)}, u32[]{:S(2)}, u32[]{:S(2)}) async-start(f32[128,8,128]{2,1,0:T(8,128)} %bitcast.34), calls=%async_computation | async-start | bytes 1048576 | tf_op jit(solution)/shard_map/all_to_all | solution.py:648
  14.5 0.0 copy-done
  14.5 0.0 copy-done.5
  14.5 1.9 %positions.1.position_ref = f32[3,128,128]{2,1,0:T(8,128)S(1)} custom-call(f32[3,4096]{1,0:T(4,128)S(1)} %copy-done.5, s32[128,128]{1,0:T(8,128)S(1)} %bitcast.23), custom_call_target="tpu_custom_call" | custom-call | flops 1000000 | bytes 1000000 | tf_op jit(solution)/shard_map/positions/pallas_call | solution.py:662
  16.5 0.0 copy-start.6
  16.5 11.7 %all-to-all-done = f32[128,8,128]{2,1,0:T(8,128)S(1)} async-done(((f32[128,8,128]{2,1,0:T(8,128)}), f32[128,8,128]{2,1,0:T(8,128)S(1)}, u32[]{:S(2)}, u32[]{:S(2)}) %all-to-all-start) | async-done | bytes 524320 | tf_op jit(solution)/shard_map/all_to_all | solution.py:648
  28.2 0.0 copy-done.6
  28.2 9.2 %eliminate.1 = f32[1024,128]{1,0:T(8,128)S(1)} custom-call(f32[1024,128]{1,0:T(8,128)S(1)} %bitcast.18, f32[3,128,128]{2,1,0:T(8,128)S(1)} %positions.1.position_ref, s32[128,128]{1,0:T(8,128)S(1)} %bitcast.24, s32[1,128]{1,0:T(1,128)S(1)} %copy-done.6), custom_call_target="tpu_custom_call" | custom-call | flops 1000000 | bytes 1000000 | tf_op jit(solution)/shard_map/eliminate/pallas_call | solution.py:663
  37.4 0.0 copy-start.1
  37.4 0.0 copy-start.2
  37.4 0.0 copy-start.3
  37.4 0.0 copy-start.4
  37.4 18.0 %all_to_all.25 = f32[128,8,128]{2,1,0:T(8,128)S(1)} all-to-all(f32[128,8,128]{2,1,0:T(8,128)S(1)} %bitcast.19), channel_id=1, replica_groups=mesh['gx'=4,'gy'=32] {'gx','gy'}, dimensions={0} | all-to-all | bytes 1048576 | tf_op jit(solution)/shard_map/all_to_all | solution.py:648
  55.5 0.0 copy-done.1
  55.5 0.0 copy-done.2
  55.5 0.0 copy-done.3
  55.5 0.0 copy-done.4
  55.5 4.3 %cameras.1 = (f32[256,128]{1,0:T(8,128)S(1)}, f32[32,256]{1,0:T(8,128)S(1)}, f32[8,256]{1,0:T(8,128)S(1)}) custom-call(f32[1024,128]{1,0:T(8,128)S(1)} %bitcast.20, s32[128,128]{1,0:T(8,128)S(1)} %bitcast.26, s32[16,128]{1,0:T(8,128)S(1)} %bitcast.30, s32[8,256]{1,0:T(8,128)S(1)} %copy-done.3, f32[8,256]{1,0:T(8,128)S(1)} %copy-done.4), custom_call_target="tpu_custom_call" | custom-call | flops 1000000 | bytes 1000000 | tf_op jit(solution)/shard_map/cameras/pallas_call | solution.py:665
  59.8 14.4 %all_to_all.26 = f32[128,2,128]{2,1,0:T(2,128)S(1)} all-to-all(f32[128,2,128]{2,1,0:T(2,128)S(1)} %bitcast.28), channel_id=1, replica_groups=mesh['gx'=4,'gy'=32] {'gx','gy'}, dimensions={0} | all-to-all | bytes 262144 | tf_op jit(solution)/shard_map/all_to_all | solution.py:648
  74.2 1.7 %first_product.1 = (f32[256,128]{1,0:T(8,128)S(1)}, f32[8,256]{1,0:T(8,128)S(1)}, f32[8,256]{1,0:T(8,128)S(1)}) custom-call(f32[256,128]{1,0:T(8,128)S(1)} %bitcast.22, f32[32,256]{1,0:T(8,128)S(1)} %get-tuple-element.11.system_ref, f32[8,256]{1,0:T(8,128)S(1)} %get-tuple-element.12.vector_ref, s32[16,128]{1,0:T(8,128)S(1)} %bitcast.31, ...), custom_call_target="tpu_custom_call" | custom-call | flops 1000000 | bytes 1000000 | tf_op jit(solution)/shard_map/first_product/pallas_call | solution.py:666
  75.9 14.3 %all_to_all.27 = f32[128,2,128]{2,1,0:T(2,128)S(1)} all-to-all(f32[128,2,128]{2,1,0:T(2,128)S(1)} %bitcast.29), channel_id=1, replica_groups=mesh['gx'=4,'gy'=32] {'gx','gy'}, dimensions={0} | all-to-all | bytes 262144 | tf_op jit(solution)/shard_map/all_to_all | solution.py:648
  90.1 0.8 second_product.1
  90.9 13.7 %all_to_all.28 = f32[128,1,128]{2,1,0:T(1,128)S(1)} all-to-all(f32[128,1,128]{2,1,0:T(1,128)S(1)} %bitcast.33), channel_id=1, replica_groups=mesh['gx'=4,'gy'=32] {'gx','gy'}, dimensions={0} | all-to-all | bytes 131072 | tf_op jit(solution)/shard_map/all_to_all | solution.py:648
  104.7 0.9 last.1
Async XLA Ops:
  2.9 11.5 %copy-start = (s32[1,128,128]{2,1,0:T(8,128)S(1)}, s32[1,128,128]{2,1,0:T(8,128)}, u32[]{:S(2)}) copy-start(s32[1,128,128]{2,1,0:T(8,128)} %param.13) | copy-start | bytes 196612
  3.0 11.5 %copy-start.5 = (f32[3,4096]{1,0:T(4,128)S(1)}, f32[3,4096]{1,0:T(4,128)}, u32[]{:S(2)}) copy-start(f32[3,4096]{1,0:T(4,128)} %points_ref.1) | copy-start | bytes 147460
  3.0 25.2 %all-to-all-start = ((f32[128,8,128]{2,1,0:T(8,128)}), f32[128,8,128]{2,1,0:T(8,128)S(1)}, u32[]{:S(2)}, u32[]{:S(2)}) async-start(f32[128,8,128]{2,1,0:T(8,128)} %bitcast.34), calls=%async_computation | async-start | bytes 1048576 | tf_op jit(solution)/shard_map/all_to_all | solution.py:648
  16.5 11.8 %copy-start.6 = (s32[1,128]{1,0:T(1,128)S(1)}, s32[1,128]{1,0:T(1,128)}, u32[]{:S(2)}) copy-start(s32[1,128]{1,0:T(1,128)} %count_ref.1) | copy-start | bytes 1540
  37.4 18.1 %copy-start.1 = (s32[1,128,128]{2,1,0:T(8,128)S(1)}, s32[1,128,128]{2,1,0:T(8,128)}, u32[]{:S(2)}) copy-start(s32[1,128,128]{2,1,0:T(8,128)} %param.12) | copy-start | bytes 196612
  37.4 18.1 %copy-start.2 = (s32[1,128,16]{1,2,0:T(8,128)S(1)}, s32[1,128,16]{1,2,0:T(8,128)}, u32[]{:S(2)}) copy-start(s32[1,128,16]{1,2,0:T(8,128)} %param.15) | copy-start | bytes 24580
  37.4 18.1 %copy-start.3 = (s32[8,256]{1,0:T(8,128)S(1)}, s32[8,256]{1,0:T(8,128)}, u32[]{:S(2)}) copy-start(s32[8,256]{1,0:T(8,128)} %edge_ref.5) | copy-start | bytes 24580
  37.4 18.1 %copy-start.4 = (f32[8,256]{1,0:T(8,128)S(1)}, f32[8,256]{1,0:T(8,128)}, u32[]{:S(2)}) copy-start(f32[8,256]{1,0:T(8,128)} %weight_ref.5) | copy-start | bytes 24580

commit v5 on v4

--- a/solution.py
+++ b/solution.py
@@ -78,7 +78,7 @@
     ]
     for copy in copies:
         copy.start()
-    for copy in copies:
+    for copy in copies[0:2]:
         copy.wait()
     inverse = 1.0 / pose_ref[0:1, :]
     pose_ref[1:4, :] = pose_ref[1:4, :] * inverse
@@ -94,11 +94,18 @@
                 take(spread(row[:, 128:256], 8), lane),
                 take(spread(row[:, 0:128], 8), lane),
             )
+        return carry
+
+    lax.fori_loop(0, 16, tile, 0, unroll=8)
+    copies[2].wait()
+
+    def measured(t, carry):
+        base = pl.multiple_of(t * 8, 8)
         for r in range(2):
             out_ref[pl.ds(base * 8 + 6 + r, 8, stride=8), :] = uv_ref[r, pl.ds(base, 8), :]
         return carry
 
-    lax.fori_loop(0, 16, tile, 0, unroll=4)
+    lax.fori_loop(0, 16, measured, 0, unroll=16)
 
 
 def position_kernel(points_ref, index_ref, out_ref):

time: 106 us -> 106 us (level)
  no operation moved by 1% of the time
where the time goes in v5:
time: 106 us; the launch traced here: 105 us
  blocking collectives  60.4 us (57%)
  Pallas kernels  20.9 us (20%)
  waiting for transfers between devices  11.7 us (11%)
  starting transfers between devices  11.5 us (11%)
    all_to_all x4, blocking collectives, swap(): lax.all_to_all(blocks, AXES, split_axis=0, concat_axis=0, tiled=True)  60.4 us
    all_to_all x1, waiting for transfers between devices, swap(): lax.all_to_all(blocks, AXES, split_axis=0, concat_axis=0, tiled=True)  11.7 us
    all_to_all x1, starting transfers between devices, swap(): lax.all_to_all(blocks, AXES, split_axis=0, concat_axis=0, tiled=True)  11.5 us
    pallas_call x1, Pallas kernels, per_device(): reduced = run['eliminate'](arrived, position, point_index, block_count)  9.15 us
    pallas_call x1, Pallas kernels, per_device(): payload, system, vector = run['cameras'](returned, cam_index, *graph)  4.31 us
  transfers between devices with their start and end apart: 1, of which 1 were waited for; matrix products, arithmetic and copies ran while one was open for 0% of the time, Pallas kernels for 2%

profile of v5, /device:TPU:1, one launch (start us, length us, event | category | flops | bytes accessed | tf_op | source)
XLA Modules:
  0.0 105.3 jit_solution(3762883465219980204)
XLA Ops:
  0.6 2.1 %poses.1 = f32[1024,128]{1,0:T(8,128)} custom-call(f32[7,256]{1,0:T(8,128)} %pose_hbm.1, s32[128,128]{1,0:T(8,128)} %bitcast.25, f32[2,128,128]{2,1,0:T(8,128)} %bitcast.35), custom_call_target="tpu_custom_call" | custom-call | flops 1000000 | bytes 1000000 | tf_op jit(solution)/shard_map/poses/pallas_call | solution.py:667
  2.7 0.0 copy-start
  2.7 0.0 copy-start.5
  2.8 11.5 %all-to-all-start = ((f32[128,8,128]{2,1,0:T(8,128)}), f32[128,8,128]{2,1,0:T(8,128)S(1)}, u32[]{:S(2)}, u32[]{:S(2)}) async-start(f32[128,8,128]{2,1,0:T(8,128)} %bitcast.34), calls=%async_computation | async-start | bytes 1048576 | tf_op jit(solution)/shard_map/all_to_all | solution.py:655
  14.3 0.0 copy-done
  14.3 0.0 copy-done.5
  14.3 1.9 %positions.1.position_ref = f32[3,128,128]{2,1,0:T(8,128)S(1)} custom-call(f32[3,4096]{1,0:T(4,128)S(1)} %copy-done.5, s32[128,128]{1,0:T(8,128)S(1)} %bitcast.23), custom_call_target="tpu_custom_call" | custom-call | flops 1000000 | bytes 1000000 | tf_op jit(solution)/shard_map/positions/pallas_call | solution.py:669
  16.2 0.0 copy-start.6
  16.2 11.7 %all-to-all-done = f32[128,8,128]{2,1,0:T(8,128)S(1)} async-done(((f32[128,8,128]{2,1,0:T(8,128)}), f32[128,8,128]{2,1,0:T(8,128)S(1)}, u32[]{:S(2)}, u32[]{:S(2)}) %all-to-all-start) | async-done | bytes 524320 | tf_op jit(solution)/shard_map/all_to_all | solution.py:655
  28.0 0.0 copy-done.6
  28.0 9.2 %eliminate.1 = f32[1024,128]{1,0:T(8,128)S(1)} custom-call(f32[1024,128]{1,0:T(8,128)S(1)} %bitcast.18, f32[3,128,128]{2,1,0:T(8,128)S(1)} %positions.1.position_ref, s32[128,128]{1,0:T(8,128)S(1)} %bitcast.24, s32[1,128]{1,0:T(1,128)S(1)} %copy-done.6), custom_call_target="tpu_custom_call" | custom-call | flops 1000000 | bytes 1000000 | tf_op jit(solution)/shard_map/eliminate/pallas_call | solution.py:670
  37.1 0.0 copy-start.1
  37.2 0.0 copy-start.2
  37.2 0.0 copy-start.3
  37.2 0.0 copy-start.4
  37.2 18.0 %all_to_all.25 = f32[128,8,128]{2,1,0:T(8,128)S(1)} all-to-all(f32[128,8,128]{2,1,0:T(8,128)S(1)} %bitcast.19), channel_id=1, replica_groups=mesh['gx'=4,'gy'=32] {'gx','gy'}, dimensions={0} | all-to-all | bytes 1048576 | tf_op jit(solution)/shard_map/all_to_all | solution.py:655
  55.2 0.0 copy-done.1
  55.2 0.0 copy-done.2
  55.2 0.0 copy-done.3
  55.3 0.0 copy-done.4
  55.3 4.3 %cameras.1 = (f32[256,128]{1,0:T(8,128)S(1)}, f32[32,256]{1,0:T(8,128)S(1)}, f32[8,256]{1,0:T(8,128)S(1)}) custom-call(f32[1024,128]{1,0:T(8,128)S(1)} %bitcast.20, s32[128,128]{1,0:T(8,128)S(1)} %bitcast.26, s32[16,128]{1,0:T(8,128)S(1)} %bitcast.30, s32[8,256]{1,0:T(8,128)S(1)} %copy-done.3, f32[8,256]{1,0:T(8,128)S(1)} %copy-done.4), custom_call_target="tpu_custom_call" | custom-call | flops 1000000 | bytes 1000000 | tf_op jit(solution)/shard_map/cameras/pallas_call | solution.py:672
  59.6 14.4 %all_to_all.26 = f32[128,2,128]{2,1,0:T(2,128)S(1)} all-to-all(f32[128,2,128]{2,1,0:T(2,128)S(1)} %bitcast.28), channel_id=1, replica_groups=mesh['gx'=4,'gy'=32] {'gx','gy'}, dimensions={0} | all-to-all | bytes 262144 | tf_op jit(solution)/shard_map/all_to_all | solution.py:655
  74.0 1.7 %first_product.1 = (f32[256,128]{1,0:T(8,128)S(1)}, f32[8,256]{1,0:T(8,128)S(1)}, f32[8,256]{1,0:T(8,128)S(1)}) custom-call(f32[256,128]{1,0:T(8,128)S(1)} %bitcast.22, f32[32,256]{1,0:T(8,128)S(1)} %get-tuple-element.11.system_ref, f32[8,256]{1,0:T(8,128)S(1)} %get-tuple-element.12.vector_ref, s32[16,128]{1,0:T(8,128)S(1)} %bitcast.31, ...), custom_call_target="tpu_custom_call" | custom-call | flops 1000000 | bytes 1000000 | tf_op jit(solution)/shard_map/first_product/pallas_call | solution.py:673
  75.7 14.3 %all_to_all.27 = f32[128,2,128]{2,1,0:T(2,128)S(1)} all-to-all(f32[128,2,128]{2,1,0:T(2,128)S(1)} %bitcast.29), channel_id=1, replica_groups=mesh['gx'=4,'gy'=32] {'gx','gy'}, dimensions={0} | all-to-all | bytes 262144 | tf_op jit(solution)/shard_map/all_to_all | solution.py:655
  89.9 0.8 second_product.1
  90.7 13.7 %all_to_all.28 = f32[128,1,128]{2,1,0:T(1,128)S(1)} all-to-all(f32[128,1,128]{2,1,0:T(1,128)S(1)} %bitcast.33), channel_id=1, replica_groups=mesh['gx'=4,'gy'=32] {'gx','gy'}, dimensions={0} | all-to-all | bytes 131072 | tf_op jit(solution)/shard_map/all_to_all | solution.py:655
  104.4 0.9 last.1
Async XLA Ops:
  2.7 11.5 %copy-start = (s32[1,128,128]{2,1,0:T(8,128)S(1)}, s32[1,128,128]{2,1,0:T(8,128)}, u32[]{:S(2)}) copy-start(s32[1,128,128]{2,1,0:T(8,128)} %param.13) | copy-start | bytes 196612
  2.7 11.5 %copy-start.5 = (f32[3,4096]{1,0:T(4,128)S(1)}, f32[3,4096]{1,0:T(4,128)}, u32[]{:S(2)}) copy-start(f32[3,4096]{1,0:T(4,128)} %points_ref.1) | copy-start | bytes 147460
  2.8 25.2 %all-to-all-start = ((f32[128,8,128]{2,1,0:T(8,128)}), f32[128,8,128]{2,1,0:T(8,128)S(1)}, u32[]{:S(2)}, u32[]{:S(2)}) async-start(f32[128,8,128]{2,1,0:T(8,128)} %bitcast.34), calls=%async_computation | async-start | bytes 1048576 | tf_op jit(solution)/shard_map/all_to_all | solution.py:655
  16.2 11.8 %copy-start.6 = (s32[1,128]{1,0:T(1,128)S(1)}, s32[1,128]{1,0:T(1,128)}, u32[]{:S(2)}) copy-start(s32[1,128]{1,0:T(1,128)} %count_ref.1) | copy-start | bytes 1540
  37.1 18.1 %copy-start.1 = (s32[1,128,128]{2,1,0:T(8,128)S(1)}, s32[1,128,128]{2,1,0:T(8,128)}, u32[]{:S(2)}) copy-start(s32[1,128,128]{2,1,0:T(8,128)} %param.12) | copy-start | bytes 196612
  37.2 18.1 %copy-start.2 = (s32[1,128,16]{1,2,0:T(8,128)S(1)}, s32[1,128,16]{1,2,0:T(8,128)}, u32[]{:S(2)}) copy-start(s32[1,128,16]{1,2,0:T(8,128)} %param.15) | copy-start | bytes 24580
  37.2 18.1 %copy-start.3 = (s32[8,256]{1,0:T(8,128)S(1)}, s32[8,256]{1,0:T(8,128)}, u32[]{:S(2)}) copy-start(s32[8,256]{1,0:T(8,128)} %edge_ref.5) | copy-start | bytes 24580
  37.2 18.1 %copy-start.4 = (f32[8,256]{1,0:T(8,128)S(1)}, f32[8,256]{1,0:T(8,128)}, u32[]{:S(2)}) copy-start(f32[8,256]{1,0:T(8,128)} %weight_ref.5) | copy-start | bytes 24580

commit v6 on v4

--- a/solution.py
+++ b/solution.py
@@ -69,7 +69,8 @@
 
 
 def pose_kernel(
-    pose_hbm, cam_hbm, uv_hbm, out_ref, pose_ref, cam_ref, uv_ref, pose_sem, cam_sem, uv_sem
+    pose_hbm, cam_hbm, uv_hbm, out_hbm, pose_ref, cam_ref, uv_ref, out_ref, pose_sem, cam_sem,
+    uv_sem, out_sem,
 ):
     copies = [
         pltpu.make_async_copy(pose_hbm, pose_ref, pose_sem),
@@ -78,13 +79,13 @@
     ]
     for copy in copies:
         copy.start()
-    for copy in copies:
+    for copy in copies[0:2]:
         copy.wait()
     inverse = 1.0 / pose_ref[0:1, :]
     pose_ref[1:4, :] = pose_ref[1:4, :] * inverse
 
-    def tile(t, carry):
-        base = pl.multiple_of(t * 8, 8)
+    def tile(t):
+        base = t * 8
         index = cam_ref[pl.ds(base, 8), :]
         lane, upper = index & 127, index >= 128
         for r in range(6):
@@ -96,9 +97,18 @@
             )
         for r in range(2):
             out_ref[pl.ds(base * 8 + 6 + r, 8, stride=8), :] = uv_ref[r, pl.ds(base, 8), :]
-        return carry
-
-    lax.fori_loop(0, 16, tile, 0, unroll=4)
+
+    def send(g):
+        rows = pl.ds(g * 512, 512)
+        return pltpu.make_async_copy(out_ref.at[rows], out_hbm.at[rows], out_sem.at[g])
+
+    copies[2].wait()
+    for g in range(2):
+        for k in range(8):
+            tile(8 * g + k)
+        send(g).start()
+    for g in range(2):
+        send(g).wait()
 
 
 def position_kernel(points_ref, index_ref, out_ref):
@@ -591,9 +601,12 @@
                 vmem((7, 256), F32),
                 vmem((128, 128), jnp.int32),
                 vmem((2, 128, 128), F32),
+                vmem((1024, 128), F32),
             ]
-            + [pltpu.SemaphoreType.DMA] * 3,
+            + [pltpu.SemaphoreType.DMA] * 3
+            + [pltpu.SemaphoreType.DMA((2,))],
             in_specs=[pl.BlockSpec(memory_space=pl.ANY)] * 3,
+            out_specs=pl.BlockSpec(memory_space=pl.ANY),
             vmem=None,
         ),
         "positions": call(position_kernel, "positions", array(3, 128, 128)),

time: 106 us -> 106 us (level)
  no operation moved by 1% of the time
where the time goes in v6:
time: 106 us; the launch traced here: 105 us
  blocking collectives  60.4 us (57%)
  Pallas kernels  20.8 us (20%)
  waiting for transfers between devices  11.7 us (11%)
  starting transfers between devices  11.5 us (11%)
    all_to_all x4, blocking collectives, swap(): lax.all_to_all(blocks, AXES, split_axis=0, concat_axis=0, tiled=True)  60.4 us
    all_to_all x1, waiting for transfers between devices, swap(): lax.all_to_all(blocks, AXES, split_axis=0, concat_axis=0, tiled=True)  11.7 us
    all_to_all x1, starting transfers between devices, swap(): lax.all_to_all(blocks, AXES, split_axis=0, concat_axis=0, tiled=True)  11.5 us
    pallas_call x1, Pallas kernels, per_device(): reduced = run['eliminate'](arrived, position, point_index, block_count)  9.16 us
    pallas_call x1, Pallas kernels, per_device(): payload, system, vector = run['cameras'](returned, cam_index, *graph)  4.31 us
  transfers between devices with their start and end apart: 1, of which 1 were waited for; matrix products, arithmetic and copies ran while one was open for 0% of the time, Pallas kernels for 2%

profile of v6, /device:TPU:1, one launch (start us, length us, event | category | flops | bytes accessed | tf_op | source)
XLA Modules:
  0.0 105.2 jit_solution(4986946502417788923)
XLA Ops:
  0.6 2.0 %poses.1 = f32[1024,128]{1,0:T(8,128)} custom-call(f32[7,256]{1,0:T(8,128)} %pose_hbm.1, s32[128,128]{1,0:T(8,128)} %bitcast.25, f32[2,128,128]{2,1,0:T(8,128)} %bitcast.35), custom_call_target="tpu_custom_call" | custom-call | flops 1000000 | bytes 1000000 | tf_op jit(solution)/shard_map/poses/pallas_call | solution.py:673
  2.7 0.0 copy-start
  2.7 0.0 copy-start.5
  2.7 11.5 %all-to-all-start = ((f32[128,8,128]{2,1,0:T(8,128)}), f32[128,8,128]{2,1,0:T(8,128)S(1)}, u32[]{:S(2)}, u32[]{:S(2)}) async-start(f32[128,8,128]{2,1,0:T(8,128)} %bitcast.34), calls=%async_computation | async-start | bytes 1048576 | tf_op jit(solution)/shard_map/all_to_all | solution.py:661
  14.2 0.0 copy-done
  14.2 0.0 copy-done.5
  14.2 1.9 %positions.1.position_ref = f32[3,128,128]{2,1,0:T(8,128)S(1)} custom-call(f32[3,4096]{1,0:T(4,128)S(1)} %copy-done.5, s32[128,128]{1,0:T(8,128)S(1)} %bitcast.23), custom_call_target="tpu_custom_call" | custom-call | flops 1000000 | bytes 1000000 | tf_op jit(solution)/shard_map/positions/pallas_call | solution.py:675
  16.2 0.0 copy-start.6
  16.2 11.7 %all-to-all-done = f32[128,8,128]{2,1,0:T(8,128)S(1)} async-done(((f32[128,8,128]{2,1,0:T(8,128)}), f32[128,8,128]{2,1,0:T(8,128)S(1)}, u32[]{:S(2)}, u32[]{:S(2)}) %all-to-all-start) | async-done | bytes 524320 | tf_op jit(solution)/shard_map/all_to_all | solution.py:661
  27.9 0.0 copy-done.6
  27.9 9.2 %eliminate.1 = f32[1024,128]{1,0:T(8,128)S(1)} custom-call(f32[1024,128]{1,0:T(8,128)S(1)} %bitcast.18, f32[3,128,128]{2,1,0:T(8,128)S(1)} %positions.1.position_ref, s32[128,128]{1,0:T(8,128)S(1)} %bitcast.24, s32[1,128]{1,0:T(1,128)S(1)} %copy-done.6), custom_call_target="tpu_custom_call" | custom-call | flops 1000000 | bytes 1000000 | tf_op jit(solution)/shard_map/eliminate/pallas_call | solution.py:676
  37.1 0.0 copy-start.1
  37.1 0.0 copy-start.2
  37.1 0.0 copy-start.3
  37.1 0.0 copy-start.4
  37.1 18.0 %all_to_all.25 = f32[128,8,128]{2,1,0:T(8,128)S(1)} all-to-all(f32[128,8,128]{2,1,0:T(8,128)S(1)} %bitcast.19), channel_id=1, replica_groups=mesh['gx'=4,'gy'=32] {'gx','gy'}, dimensions={0} | all-to-all | bytes 1048576 | tf_op jit(solution)/shard_map/all_to_all | solution.py:661
  55.2 0.0 copy-done.1
  55.2 0.0 copy-done.2
  55.2 0.0 copy-done.3
  55.2 0.0 copy-done.4
  55.2 4.3 %cameras.1 = (f32[256,128]{1,0:T(8,128)S(1)}, f32[32,256]{1,0:T(8,128)S(1)}, f32[8,256]{1,0:T(8,128)S(1)}) custom-call(f32[1024,128]{1,0:T(8,128)S(1)} %bitcast.20, s32[128,128]{1,0:T(8,128)S(1)} %bitcast.26, s32[16,128]{1,0:T(8,128)S(1)} %bitcast.30, s32[8,256]{1,0:T(8,128)S(1)} %copy-done.3, f32[8,256]{1,0:T(8,128)S(1)} %copy-done.4), custom_call_target="tpu_custom_call" | custom-call | flops 1000000 | bytes 1000000 | tf_op jit(solution)/shard_map/cameras/pallas_call | solution.py:678
  59.5 14.4 %all_to_all.26 = f32[128,2,128]{2,1,0:T(2,128)S(1)} all-to-all(f32[128,2,128]{2,1,0:T(2,128)S(1)} %bitcast.28), channel_id=1, replica_groups=mesh['gx'=4,'gy'=32] {'gx','gy'}, dimensions={0} | all-to-all | bytes 262144 | tf_op jit(solution)/shard_map/all_to_all | solution.py:661
  73.9 1.7 %first_product.1 = (f32[256,128]{1,0:T(8,128)S(1)}, f32[8,256]{1,0:T(8,128)S(1)}, f32[8,256]{1,0:T(8,128)S(1)}) custom-call(f32[256,128]{1,0:T(8,128)S(1)} %bitcast.22, f32[32,256]{1,0:T(8,128)S(1)} %get-tuple-element.11.system_ref, f32[8,256]{1,0:T(8,128)S(1)} %get-tuple-element.12.vector_ref, s32[16,128]{1,0:T(8,128)S(1)} %bitcast.31, ...), custom_call_target="tpu_custom_call" | custom-call | flops 1000000 | bytes 1000000 | tf_op jit(solution)/shard_map/first_product/pallas_call | solution.py:679
  75.6 14.3 %all_to_all.27 = f32[128,2,128]{2,1,0:T(2,128)S(1)} all-to-all(f32[128,2,128]{2,1,0:T(2,128)S(1)} %bitcast.29), channel_id=1, replica_groups=mesh['gx'=4,'gy'=32] {'gx','gy'}, dimensions={0} | all-to-all | bytes 262144 | tf_op jit(solution)/shard_map/all_to_all | solution.py:661
  89.9 0.8 second_product.1
  90.7 13.7 %all_to_all.28 = f32[128,1,128]{2,1,0:T(1,128)S(1)} all-to-all(f32[128,1,128]{2,1,0:T(1,128)S(1)} %bitcast.33), channel_id=1, replica_groups=mesh['gx'=4,'gy'=32] {'gx','gy'}, dimensions={0} | all-to-all | bytes 131072 | tf_op jit(solution)/shard_map/all_to_all | solution.py:661
  104.4 0.9 last.1
Async XLA Ops:
  2.7 11.5 %copy-start = (s32[1,128,128]{2,1,0:T(8,128)S(1)}, s32[1,128,128]{2,1,0:T(8,128)}, u32[]{:S(2)}) copy-start(s32[1,128,128]{2,1,0:T(8,128)} %param.13) | copy-start | bytes 196612
  2.7 11.5 %copy-start.5 = (f32[3,4096]{1,0:T(4,128)S(1)}, f32[3,4096]{1,0:T(4,128)}, u32[]{:S(2)}) copy-start(f32[3,4096]{1,0:T(4,128)} %points_ref.1) | copy-start | bytes 147460
  2.7 25.2 %all-to-all-start = ((f32[128,8,128]{2,1,0:T(8,128)}), f32[128,8,128]{2,1,0:T(8,128)S(1)}, u32[]{:S(2)}, u32[]{:S(2)}) async-start(f32[128,8,128]{2,1,0:T(8,128)} %bitcast.34), calls=%async_computation | async-start | bytes 1048576 | tf_op jit(solution)/shard_map/all_to_all | solution.py:661
  16.2 11.8 %copy-start.6 = (s32[1,128]{1,0:T(1,128)S(1)}, s32[1,128]{1,0:T(1,128)}, u32[]{:S(2)}) copy-start(s32[1,128]{1,0:T(1,128)} %count_ref.1) | copy-start | bytes 1540
  37.1 18.1 %copy-start.1 = (s32[1,128,128]{2,1,0:T(8,128)S(1)}, s32[1,128,128]{2,1,0:T(8,128)}, u32[]{:S(2)}) copy-start(s32[1,128,128]{2,1,0:T(8,128)} %param.12) | copy-start | bytes 196612
  37.1 18.1 %copy-start.2 = (s32[1,128,16]{1,2,0:T(8,128)S(1)}, s32[1,128,16]{1,2,0:T(8,128)}, u32[]{:S(2)}) copy-start(s32[1,128,16]{1,2,0:T(8,128)} %param.15) | copy-start | bytes 24580
  37.1 18.1 %copy-start.3 = (s32[8,256]{1,0:T(8,128)S(1)}, s32[8,256]{1,0:T(8,128)}, u32[]{:S(2)}) copy-start(s32[8,256]{1,0:T(8,128)} %edge_ref.5) | copy-start | bytes 24580
  37.1 18.1 %copy-start.4 = (f32[8,256]{1,0:T(8,128)S(1)}, f32[8,256]{1,0:T(8,128)}, u32[]{:S(2)}) copy-start(f32[8,256]{1,0:T(8,128)} %weight_ref.5) | copy-start | bytes 24580
